TPU v7x, 256 devices: a whole 4x4x8 slice. The times are simulated.
256 devices in a mesh: seq: 128 (over z_lo, x, y, core), chan: 2 (over z_hi).
Axes of the slice: x: 4, y: 4, z: 8 (z_hi: 2, z_lo: 4; z = z_hi * 4 + z_lo), core: 2. Of those that a mesh axis runs over, the one named last changes fastest.
Arguments:
- projected: float32 [3, 4096, 16384], P(None, 'chan', 'seq'), may hold values from -6 to 6
- short_taps: float32 [3, 4096, 3], P(None, 'chan'), may hold values from -4 to 4
- filters: float32 [4096, 16384], P('chan', 'seq'), may hold values from -1.5 to 1.5
- skip_gain: float32 [4096], P('chan'), may hold values from -4 to 4
- w_out: bfloat16 [4096, 2, 2048], P(None, 'chan', 'seq'), may hold values from -0.09375 to 0.09375
Outputs:
- mixed_out: float32 [16384, 4096], P('seq', 'chan')
All inputs are finite; a program needn't handle non-finite values.
Results may differ from a plain program's by a relative error of at most 0.0029.
Values may be sent and summed in bfloat16 or wider, within the bound.
No kernel may reach another device: no remote copies, remote signals or barrier semaphores. Data moves between devices by JAX's collectives and lax.ppermute only.
A program may use at most 128 MiB of HBM per device.

v0:
```python
import math

import jax
import jax.numpy as jnp
from jax import lax
from jax.sharding import PartitionSpec as P

highest = lax.Precision.HIGHEST


def from_behind(shard, axis, by):
    length = lax.axis_size(axis)
    pairs = [(i, i + by) for i in range(length) if 0 <= i + by < length]
    return lax.ppermute(shard, axis, pairs)


def dft_tables(count):
    index = jnp.arange(count, dtype=jnp.int32)
    phase = index[:, None] * index[None, :] % count
    angle = phase.astype(jnp.float32) * (2.0 * math.pi / count)
    return (jnp.cos(angle), jnp.sin(angle))


def twiddle_tables(rows, width):
    total = rows * width
    phase = (
        jnp.arange(rows, dtype=jnp.int32)[:, None]
        * jnp.arange(width, dtype=jnp.int32)[None, :]
        % total
    )
    angle = phase.astype(jnp.float32) * (2.0 * math.pi / total)
    return (jnp.cos(angle), jnp.sin(angle))


def forward_spectrum(signal, rows):
    width = signal.shape[2]
    cos_rows, sin_rows = dft_tables(rows)
    first_re = jnp.einsum("kn,bnj->bkj", cos_rows, signal, precision=highest)
    first_im = -jnp.einsum("kn,bnj->bkj", sin_rows, signal, precision=highest)
    tw_cos, tw_sin = twiddle_tables(rows, width)
    second_re = first_re * tw_cos + first_im * tw_sin
    second_im = first_im * tw_cos - first_re * tw_sin
    cos_cols, sin_cols = dft_tables(width)
    stacked = jnp.concatenate([second_re, second_im], axis=2)
    out_re = jnp.einsum(
        "bkj,jl->bkl", stacked, jnp.concatenate([cos_cols, sin_cols], axis=0), precision=highest
    )
    out_im = jnp.einsum(
        "bkj,jl->bkl", stacked, jnp.concatenate([-sin_cols, cos_cols], axis=0), precision=highest
    )
    return (out_re, out_im)


def inverse_signal(spec_re, spec_im, rows):
    width = spec_re.shape[2]
    cos_cols, sin_cols = dft_tables(width)
    stacked = jnp.concatenate([spec_re, spec_im], axis=2)
    mid_re = jnp.einsum(
        "bkj,jl->bkl", stacked, jnp.concatenate([cos_cols, -sin_cols], axis=0), precision=highest
    )
    mid_im = jnp.einsum(
        "bkj,jl->bkl", stacked, jnp.concatenate([sin_cols, cos_cols], axis=0), precision=highest
    )
    tw_cos, tw_sin = twiddle_tables(rows, width)
    turned_re = mid_re * tw_cos - mid_im * tw_sin
    turned_im = mid_re * tw_sin + mid_im * tw_cos
    cos_rows, sin_rows = dft_tables(rows)
    result = jnp.einsum("nk,bkj->bnj", cos_rows, turned_re, precision=highest)
    result = result - jnp.einsum("nk,bkj->bnj", sin_rows, turned_im, precision=highest)
    return result / float(rows * width)


def convolve(pieces):
    gated_part, kernel_part = pieces
    count = gated_part.shape[1]
    seq_len = gated_part.shape[2]
    rows = lax.axis_size("seq")
    width = 2 * seq_len // rows
    signals = jnp.concatenate([gated_part[0], kernel_part[0]], axis=0)
    padded = jnp.concatenate([signals, jnp.zeros_like(signals)], axis=1)
    spec_re, spec_im = forward_spectrum(padded.reshape(2 * count, rows, width), rows)
    prod_re = spec_re[:count] * spec_re[count:] - spec_im[:count] * spec_im[count:]
    prod_im = spec_re[:count] * spec_im[count:] + spec_im[:count] * spec_re[count:]
    result = inverse_signal(prod_re, prod_im, rows)[:, : rows // 2]
    result = result.reshape(1, count, seq_len)
    return lax.all_to_all(result, "seq", split_axis=2, concat_axis=0, tiled=True)


def body(projected, short_taps, filters, skip_gain, w_out):
    count = projected.shape[2]
    lead = from_behind(projected[:, :, count - 2 :], "seq", 1)
    extended = jnp.concatenate([lead, projected], axis=2)
    mixed = (
        short_taps[:, :, 0:1] * projected
        + short_taps[:, :, 1:2] * extended[:, :, 1 : count + 1]
        + short_taps[:, :, 2:3] * extended[:, :, 0:count]
    )
    gated = mixed[1] * mixed[2]
    groups = lax.axis_size("seq")
    slab = gated.shape[0]
    per_device = slab // groups
    convolved = convolve(
        (
            lax.all_to_all(
                gated.reshape(groups, per_device, count),
                "seq",
                split_axis=0,
                concat_axis=2,
                tiled=True,
            ),
            lax.all_to_all(
                filters.reshape(groups, per_device, count),
                "seq",
                split_axis=0,
                concat_axis=2,
                tiled=True,
            ),
        )
    )
    convolved = convolved.reshape(slab, count)
    features = ((convolved + skip_gain[:, None] * gated) * mixed[0]).astype(jnp.bfloat16)
    halves = lax.all_to_all(w_out, "chan", split_axis=0, concat_axis=1, tiled=True)
    piece = lax.all_gather(halves, "seq", axis=2, tiled=True)
    flat = piece.reshape(piece.shape[0], -1)
    product = lax.dot_general(
        features, flat, (((0,), (0,)), ((), ())), preferred_element_type=jnp.float32
    )
    partial_out = product.reshape(product.shape[0], piece.shape[1], piece.shape[2])
    result = lax.psum_scatter(partial_out, "chan", scatter_dimension=1, tiled=True)
    return result.reshape(result.shape[0], -1)


def solution(mesh):
    in_specs = (
        P(None, "chan", "seq"),
        P(None, "chan", None),
        P("chan", "seq"),
        P("chan"),
        P(None, "chan", "seq"),
    )
    out_specs = P("seq", "chan")
    return jax.shard_map(body, mesh=mesh, in_specs=in_specs, out_specs=out_specs, check_vma=False)
```

profile of v0, /device:TPU:1, one launch (start us, length us, event | category | flops | bytes accessed | tf_op | source)
XLA Modules:
  0.0 429.0 jit_solution(6532063991583413450)
XLA Ops:
  10.2 16.5 %all_to_all.63 = bf16[2,2,16384]{2,1,0:T(2,128)(2,1)S(1)} all-to-all(bf16[2,2,16384]{2,1,0:T(2,128)(2,1)S(1)} %reshape.86), channel_id=1, replica_groups=mesh['seq'=128,'chan'=2] {'chan'}, dimensions={0} | all-to-all | bytes 262144 | tf_op jit(solution)/shard_map/all_to_all | solution.py:122
  30.8 12.0 %all-to-all-start.1 = ((f32[128,16,128]{2,1,0:T(8,128)}), f32[128,16,128]{2,1,0:T(8,128)}, u32[]{:S(2)}, u32[]{:S(2)}) async-start(f32[128,16,128]{2,1,0:T(8,128)} %bitcast.3), calls=%async_computation.1 | async-start | bytes 2097152 | tf_op jit(solution)/shard_map/all_to_all | solution.py:111
  42.8 2.8 slice.48
  47.1 3.5 collective-permute-start
  55.4 11.2 %fusion.12 = f32[3,2048,128]{2,1,0:T(8,128)S(1)} fusion(f32[3,2048,2]{2,1,0:T(8,128)} %copy.40, f32[3,2048,128]{2,1,0:T(8,128)} %param.5, f32[3,2048]{1,0:T(4,128)S(1)} %get-tuple-element.12, f32[3,2048]{1,0:T(4,128)S(1)} %get-tuple-element.13, f32[3,2048]{1,0:T(4,128)S(1)} %bitcast.108), kind=kLoop, calls=%fused_computation.22 | loop fusion | flops 5505024 | bytes 6414336 | tf_op jit(solution)/shard_map/add | solution.py:94
  67.8 6.8 %all-to-all-done.1 = f32[128,16,128]{2,1,0:T(8,128)} async-done(((f32[128,16,128]{2,1,0:T(8,128)}), f32[128,16,128]{2,1,0:T(8,128)}, u32[]{:S(2)}, u32[]{:S(2)}) %all-to-all-start.1) | async-done | bytes 1048608 | tf_op jit(solution)/shard_map/all_to_all | solution.py:111
  74.6 16.8 %all-to-all-start = ((f32[128,16,128]{2,1,0:T(8,128)}), f32[128,16,128]{2,1,0:T(8,128)}, u32[]{:S(2)}, u32[]{:S(2)}) async-start(f32[128,16,128]{2,1,0:T(8,128)} %bitcast.102), calls=%async_computation | async-start | bytes 2097152 | tf_op jit(solution)/shard_map/all_to_all | solution.py:104
  99.8 23.3 %all-to-all-done = f32[128,16,128]{2,1,0:T(8,128)} async-done(((f32[128,16,128]{2,1,0:T(8,128)}), f32[128,16,128]{2,1,0:T(8,128)}, u32[]{:S(2)}, u32[]{:S(2)}) %all-to-all-start) | async-done | bytes 1048608 | tf_op jit(solution)/shard_map/all_to_all | solution.py:104
  127.1 6.9 %fusion.61 = f32[32,256,128]{2,1,0:T(8,128)S(1)} fusion(f32[32,128,256]{2,1,0:T(8,128)S(1)} %bitcast.97), kind=kOutput, calls=%fused_computation.87 | convolution fusion | flops 1610842112 | bytes 8388608 | tf_op jit(solution)/shard_map/kn,bnj->bkj/dot_general | solution.py:39
  134.0 7.6 %fusion.5 = (f32[32,128,256]{1,2,0:T(8,128)S(1)}, f32[32,128,256]{1,2,0:T(8,128)S(1)}) fusion(f32[32,256,128]{2,1,0:T(8,128)S(1)} %fusion.61, f32[128,256]{0,1:T(8,128)S(1)} %copy-done.5, f32[128,256]{0,1:T(8,128)S(1)} %copy-done.7, f32[32,128,256]{2,1,0:T(8,128)S(1)} %bitcast.98), kind=kOutput, calls=%fused_computation.13 | convolution fusion | flops 1618182144 | bytes 17039360 | tf_op jit(solution)/shard_map/kn,bnj->bkj/dot_general | solution.py:38
  141.6 14.3 %fusion.3 = f32[32,128,256]{2,1,0:T(8,128)S(1)} fusion(f32[32,128,256]{1,2,0:T(8,128)S(1)} %get-tuple-element.6, f32[32,128,256]{1,2,0:T(8,128)S(1)} %get-tuple-element.5, f32[256,256]{1,0:T(8,128)S(1)} %get-tuple-element.16, f32[256,256]{1,0:T(8,128)S(1)} %copy-done.2), kind=kOutput, calls=%fused_computation.4 | convolution fusion | flops 6444679168 | bytes 13107200 | tf_op jit(solution)/shard_map/bkj,jl->bkl/dot_general | solution.py:48
  155.9 14.5 %fusion.4 = f32[32,128,256]{2,1,0:T(8,128)S(1)} fusion(f32[32,128,256]{1,2,0:T(8,128)S(1)} %get-tuple-element.6, f32[32,128,256]{1,2,0:T(8,128)S(1)} %get-tuple-element.5, f32[256,256]{1,0:T(8,128)S(1)} %get-tuple-element.16, f32[256,256]{1,0:T(8,128)S(1)} %copy-done.1), kind=kOutput, calls=%fused_computation.5 | convolution fusion | flops 6444679168 | bytes 13107200 | tf_op jit(solution)/shard_map/bkj,jl->bkl/dot_general | solution.py:45
  171.1 3.8 fusion.8
  175.0 3.7 fusion.7
  181.1 2.7 multiply_bitcast_fusion
  184.9 6.0 %copy.61 = f32[16,64,256]{0,2,1:T(8,128)} copy(f32[16,64,256]{2,1,0:T(8,128)} %slice.68) | data formatting | bytes 2097152 | tf_op jit(solution)/shard_map/reshape | solution.py:85
  191.4 74.6 %reduce.1 = f32[16384,16]{1,0:T(8,128)} reduce(f32[16384,1,16]{2,1,0:T(1,128)} %bitcast.99, f32[]{:T(128)} %broadcast.163), dimensions={1}, to_apply=%bitcast.88.reduce_sub_computation | reduce | bytes 2097156
  266.1 6.9 %reshape.88 = f32[128,1,2048]{2,1,0:T(1,128)} reshape(f32[16384,16]{1,0:T(8,128)} %reduce.1) | data formatting | bytes 2097152
  273.0 41.8 %all_to_all.64 = f32[128,1,2048]{2,1,0:T(1,128)} all-to-all(f32[128,1,2048]{2,1,0:T(1,128)} %reshape.88), channel_id=1, replica_groups=mesh['seq'=128,'chan'=2] {'seq'}, dimensions={0} | all-to-all | bytes 2097152 | tf_op jit(solution)/shard_map/all_to_all | solution.py:86
  314.8 5.3 %reduce.2 = f32[128,2048]{1,0:T(8,128)} reduce(f32[128,1,2048]{2,1,0:T(1,128)} %all_to_all.64, f32[]{:T(128)} %broadcast.163), dimensions={1}, to_apply=%all_to_all.52.reduce_sub_computation | reduce | bytes 2097156 | tf_op jit(solution)/shard_map/all_to_all | solution.py:86
  320.1 18.2 %reshape.89 = f32[16384,1,16]{2,1,0:T(1,128)} reshape(f32[128,2048]{1,0:T(8,128)} %reduce.2) | data formatting | bytes 2097152
  338.3 6.2 %copy.50 = f32[128,1,16,128]{3,2,0,1:T(8,128)} copy(f32[128,1,16,128]{2,3,0,1:T(8,128)} %bitcast.100) | data formatting | bytes 2097152 | tf_op jit(solution)/shard_map/all_to_all | solution.py:86
  346.9 17.6 %fusion = f32[128,2,2048]{2,0,1:T(8,128)} fusion(bf16[2048,2,1,2048]{0,1,2,3:T(2,128)(2,1)} %all-gather.3.cloned.1.call-done, bf16[1,2048,128]{2,1,0:T(8,128)(2,1)} %fusion.24), kind=kOutput, calls=%fused_computation | convolution fusion | flops 2147483648 | bytes 19398656 | tf_op jit(solution)/shard_map/dot_general | solution.py:125
  364.5 57.3 %reduce-scatter.2.cloned.1.call-done = f32[128,1,2048]{2,0,1:T(8,128)} async-done(((f32[128,2,2048]{2,0,1:T(8,128)}), f32[128,1,2048]{2,0,1:T(8,128)}) %reduce-scatter.2.cloned.1.call-update) | async-done | bytes 1048592 | tf_op jit(solution)/shard_map/reduce_scatter | solution.py:129
  (55 shorter events, 34.6 us)
Async XLA Ops:
  6.5 340.4 %all-gather.3.cloned.1.call-start = ((), (), s32[]{:S(2)}) async-start(), calls=%async_computation.6 | async-start | bytes 16908288 | tf_op jit(solution)/shard_map/all_gather | solution.py:123
  30.8 43.8 %all-to-all-start.1 = ((f32[128,16,128]{2,1,0:T(8,128)}), f32[128,16,128]{2,1,0:T(8,128)}, u32[]{:S(2)}, u32[]{:S(2)}) async-start(f32[128,16,128]{2,1,0:T(8,128)} %bitcast.3), calls=%async_computation.1 | async-start | bytes 2097152 | tf_op jit(solution)/shard_map/all_to_all | solution.py:111
  45.6 5.0 %copy-start.8 = (f32[3,2048,3]{1,2,0:T(4,128)S(1)}, f32[3,2048,3]{1,2,0:T(4,128)}, u32[]{:S(2)}) copy-start(f32[3,2048,3]{1,2,0:T(4,128)} %param.6) | copy-start | bytes 221188
  47.1 6.2 %collective-permute-start = (f32[3,2048,2]{1,0,2:T(4,128)S(1)}, f32[3,2048,2]{1,0,2:T(4,128)S(1)}, u32[]{:S(2)}, u32[]{:S(2)}) collective-permute-start(f32[3,2048,2]{1,0,2:T(4,128)S(1)} %copy.66), channel_id=1, source_target_pairs={{0,2},{2,4},{4,6},{6,8},{8,10},{10,12},{12,14},{14,16},{16,18},{18... | collective-permute-start | bytes 147464 | tf_op jit(solution)/shard_map/ppermute | solution.py:14
  74.6 48.5 %all-to-all-start = ((f32[128,16,128]{2,1,0:T(8,128)}), f32[128,16,128]{2,1,0:T(8,128)}, u32[]{:S(2)}, u32[]{:S(2)}) async-start(f32[128,16,128]{2,1,0:T(8,128)} %bitcast.102), calls=%async_computation | async-start | bytes 2097152 | tf_op jit(solution)/shard_map/all_to_all | solution.py:104
  91.4 330.4 %reduce-scatter.2.cloned.1.call-start = ((), (), s32[]{:S(2)}) async-start(), calls=%async_computation.5 | async-start | bytes 3145728 | tf_op jit(solution)/shard_map/reduce_scatter | solution.py:129
  91.9 0.9 copy-start.4
  92.0 0.9 copy-start.6
  123.1 2.3 copy-start
  127.1 6.9 %copy-start.5 = (f32[128,256]{0,1:T(8,128)S(1)}, f32[128,256]{0,1:T(8,128)}, u32[]{:S(2)}) copy-start(f32[128,256]{0,1:T(8,128)} %copy-done.4) | copy-start | bytes 393220
  127.1 6.9 %copy-start.7 = (f32[128,256]{0,1:T(8,128)S(1)}, f32[128,256]{0,1:T(8,128)}, u32[]{:S(2)}) copy-start(f32[128,256]{0,1:T(8,128)} %copy-done.6) | copy-start | bytes 393220
  134.0 7.6 %copy-start.2 = (f32[256,256]{1,0:T(8,128)S(1)}, f32[256,256]{1,0:T(8,128)}, u32[]{:S(2)}) copy-start(f32[256,256]{1,0:T(8,128)} %get-tuple-element.17) | copy-start | bytes 786436
  141.6 14.3 %copy-start.1 = (f32[256,256]{1,0:T(8,128)S(1)}, f32[256,256]{1,0:T(8,128)}, u32[]{:S(2)}) copy-start(f32[256,256]{1,0:T(8,128)} %fusion.51) | copy-start | bytes 786436
  175.0 3.7 copy-start.3
  338.3 6.2 %copy-start.9 = (f32[2048]{0:T(1024)S(1)}, f32[2048]{0:T(1024)}, u32[]{:S(2)}) copy-start(f32[2048]{0:T(1024)} %param.8) | copy-start | bytes 24580
Sparse Core Ops, SparseCore 0:
  30.9 235.2 all-gather.2
  364.6 57.0 reduce-scatter.1
where the time goes:
time: 438 us; the launch traced here: 429 us
  other arithmetic  102 us (23%)
  waiting for transfers between devices  89.9 us (21%)
  matrix products  73.5 us (17%)
  local copies, waits for them, and re-layouts  59.1 us (13%)
  blocking collectives  58.3 us (13%)
  starting transfers between devices  32.4 us (7%)
  between operations  14.2 us (3%)
    unnamed x2, other arithmetic  76.2 us
    reduce_scatter x1, waiting for transfers between devices, body(): lax.psum_scatter(partial_out, 'chan', scatter_dimension=1, tiled=True)  57.3 us
    all_to_all x1, blocking collectives, convolve(): lax.all_to_all(result, 'seq', split_axis=2, concat_axis=0, tiled=True)  41.8 us
    unnamed x33, local copies, waits for them, and re-layouts  34.1 us
    all_to_all x1, waiting for transfers between devices, body(): lax.all_to_all(gated.reshape(groups, per_device, count), 'seq', split_axi...  23.3 us
    dot_general x1, matrix products, body(): lax.dot_general(features, flat, (((0,), (0,)), ((), ())), preferred_eleme...  17.6 us
    all_to_all x1, starting transfers between devices, body(): lax.all_to_all(gated.reshape(groups, per_device, count), 'seq', split_axi...  16.8 us
    all_to_all x1, blocking collectives, body(): lax.all_to_all(w_out, 'chan', split_axis=0, concat_axis=1, tiled=True)  16.5 us
  transfers between devices with their start and end apart: 5, of which 4 were waited for; matrix products, arithmetic and copies ran while one was open for 49% of the time, Pallas kernels for 0%

commit v1 on v0

v1 whole, which is shorter than its diff:
```python
import math

import jax
import jax.numpy as jnp
import numpy as np
import ml_dtypes
from jax import lax
from jax.experimental import pallas as pl
from jax.experimental.pallas import tpu as pltpu
from jax.sharding import Mesh, PartitionSpec as P

BLK = 128
SEQ = ("z", "x", "y", "core")
IN_SCALE = 2.0 ** 13
H_SCALE = 2.0 ** 15
f32 = jnp.float32
bf16 = jnp.bfloat16
f16 = jnp.float16


def split_np(m):
    hi = m.astype(np.float32).astype(ml_dtypes.bfloat16)
    lo = (m - hi.astype(np.float64)).astype(np.float32).astype(ml_dtypes.bfloat16)
    return hi, lo


def tables():
    n = BLK * BLK
    k1 = np.arange(BLK)[:, None] + 0.25
    a = np.arange(BLK)[None, :]
    alpha = 2.0 * np.pi * a * k1 / BLK
    fwd_rows = np.concatenate([np.cos(alpha), np.sin(alpha)], axis=0)
    hi, lo = split_np(fwd_rows)
    rows_in = np.concatenate([hi, hi, lo], axis=1)
    tw = 2.0 * np.pi * a * k1 / n
    twiddle = np.concatenate([np.cos(tw), np.sin(tw)], axis=1).astype(np.float32)
    beta = 2.0 * np.pi * ((np.arange(BLK)[:, None] * a) % BLK) / BLK
    c, s = np.cos(beta), np.sin(beta)
    hi, lo = split_np(np.block([[c, s], [-s, c]]))
    cols_in = np.concatenate([hi, hi, lo], axis=0)
    hi, lo = split_np(np.block([[c, -s], [s, c]]))
    cols_out = np.concatenate([hi, hi, lo], axis=0)
    back = np.concatenate([np.cos(alpha).T, np.sin(alpha).T], axis=1) / (n * H_SCALE)
    hi, lo = split_np(back)
    rows_out = np.concatenate([hi, hi, lo], axis=1)
    return rows_in, twiddle, cols_in, cols_out, rows_out


def split(x):
    hi = x.astype(bf16)
    lo = (x - hi.astype(f32)).astype(bf16)
    return hi, lo


def dot(a, b):
    return jnp.dot(a, b, preferred_element_type=f32)


def conv_kernel(rows, width, taps, skip, x, e_in, tw, c_in, c_out, e_out, out, feat):
    lane = lax.broadcasted_iota(jnp.int32, (BLK, BLK), 1)
    row = lax.broadcasted_iota(jnp.int32, (BLK, BLK), 0)
    first = row == 0
    cos, sin = tw[:, :BLK], tw[:, BLK:]

    def back(p, by):
        r = pltpu.roll(p, by, 1)
        s = jnp.where(first, 0.0, pltpu.roll(r, 1, 0))
        return jnp.where(lane < by, s, r)

    def mix(i, c):
        p = x[pl.ds(i * rows + c, BLK, stride=4 * rows), :]
        t = (i * rows + c) * 3
        return taps[t] * p + taps[t + 1] * back(p, 1) + taps[t + 2] * back(p, 2)

    def step(it, carry):
        chans = [it * width + j for j in range(width)]
        gates = []
        pieces = []
        for c in chans:
            gate = mix(1, c) * mix(2, c)
            gates.append(gate)
            pieces += [gate, x[pl.ds(3 * rows + c, BLK, stride=4 * rows), :]]
        hi, lo = split(jnp.concatenate(pieces, axis=1))
        s = dot(e_in[...], jnp.concatenate([hi, lo, hi], axis=0))
        turned = []
        for j in range(2 * width):
            sr = s[:BLK, j * BLK : (j + 1) * BLK]
            si = s[BLK:, j * BLK : (j + 1) * BLK]
            turned.append(jnp.concatenate([sr * cos - si * sin, sr * sin + si * cos], axis=1))
        hi, lo = split(jnp.concatenate(turned, axis=0))
        spec = dot(jnp.concatenate([hi, lo, hi], axis=1), c_in[...])
        prods = []
        for j in range(width):
            g = spec[2 * j * BLK : (2 * j + 1) * BLK]
            h = spec[(2 * j + 1) * BLK : (2 * j + 2) * BLK]
            gr, gi, hr, hm = g[:, :BLK], g[:, BLK:], h[:, :BLK], h[:, BLK:]
            prods.append(jnp.concatenate([gr * hr - gi * hm, gr * hm + gi * hr], axis=1))
        hi, lo = split(jnp.concatenate(prods, axis=0))
        v = dot(jnp.concatenate([hi, lo, hi], axis=1), c_out[...])
        us = []
        for j in range(width):
            vr, vi = v[j * BLK : (j + 1) * BLK, :BLK], v[j * BLK : (j + 1) * BLK, BLK:]
            us.append(jnp.concatenate([vr * cos + vi * sin, vi * cos - vr * sin], axis=0))
        hi, lo = split(jnp.concatenate(us, axis=1))
        y = dot(e_out[...], jnp.concatenate([hi, lo, hi], axis=0))
        for j, c in enumerate(chans):
            f = (y[:, j * BLK : (j + 1) * BLK] + skip[c] * gates[j]) * mix(0, c)
            feat[pl.ds(c, BLK, stride=rows), :] = f
        return carry

    lax.fori_loop(0, rows // width, step, 0)
    done = feat[...].reshape(BLK, rows, BLK).astype(bf16)
    out[0] = done
    out[1] = done


def conv_features(x, taps, skip, rows):
    vmem = pl.BlockSpec(memory_space=pltpu.VMEM)
    smem = pl.BlockSpec(memory_space=pltpu.SMEM)
    consts = [jnp.asarray(t) for t in tables()]
    return pl.pallas_call(
        lambda *refs: conv_kernel(rows, 2, *refs),
        out_shape=jax.ShapeDtypeStruct((2, BLK, rows, BLK), bf16),
        in_specs=[smem, smem] + [vmem] * 6,
        out_specs=vmem,
        scratch_shapes=[pltpu.VMEM((BLK * rows, BLK), f32)],
        compiler_params=pltpu.CompilerParams(vmem_limit_bytes=40 * 2**20),
        name="conv_features",
    )(taps, skip, x.reshape(BLK * 4 * rows, BLK), *consts)


def proj_kernel(own, other, w, out_own, out_other, both):
    @pl.when((pl.program_id(0) == 0) & (pl.program_id(1) == 0))
    def _():
        both[:, :BLK] = own[...]
        both[:, BLK:] = other[...]

    wb = w[...]
    t = dot(wb.reshape(wb.shape[0] * wb.shape[2], wb.shape[3]), both[...])
    out_own[...] = t[:, :BLK].T
    out_other[...] = t[:, BLK:].T


def project(own, other, w):
    chips, halves, cols, depth = w.shape
    per = 8
    whole = pl.BlockSpec((depth, BLK), lambda i, j: (0, 0))
    out = pl.BlockSpec((BLK, per * cols), lambda i, j: (0, i * (chips // per) + j))
    shape = jax.ShapeDtypeStruct((BLK, chips * halves * cols), f32)
    return pl.pallas_call(
        proj_kernel,
        grid=(halves, chips // per),
        out_shape=(shape, shape),
        in_specs=[whole, whole, pl.BlockSpec((per, 1, cols, depth), lambda i, j: (j, i, 0, 0))],
        out_specs=(out, out),
        scratch_shapes=[pltpu.VMEM((depth, 2 * BLK), bf16)],
        compiler_params=pltpu.CompilerParams(vmem_limit_bytes=40 * 2**20),
        name="project",
    )(own, other, w)


def gather_weights(w_out):
    depth = w_out.shape[0]
    wt = w_out.reshape(depth, -1).T
    cols = wt.shape[0]
    z = lax.axis_index("z")
    mine = jnp.zeros((4, cols, depth), bf16)
    for k in range(4):
        pairs = []
        for zs in range(4):
            for cs in range(2):
                i = (zs % 2) * 2 + cs
                pairs.append((zs * 2 + cs, ((i + k) % 4) * 2 + zs // 2))
        part = lax.ppermute(wt, ("z", "core"), pairs)
        mine = lax.dynamic_update_slice(mine, part[None], ((z - k) % 4, 0, 0))
    got = lax.all_gather(mine.reshape(2, 2 * cols, depth), ("x", "y"))
    return got


def body(projected, short_taps, filters, skip_gain, w_out):
    slab, count = filters.shape
    groups = lax.axis_size(SEQ)
    rows = slab // groups
    me = lax.axis_index(SEQ)
    core = lax.axis_index("core")
    w = gather_weights(w_out)
    taps = lax.dynamic_slice(short_taps, (0, me * rows, 0), (3, rows, 3)).reshape(-1) / IN_SCALE
    skip = lax.dynamic_slice(skip_gain, (me * rows,), (rows,))
    p16 = (projected * IN_SCALE).astype(f16).reshape(3, groups, rows, count)
    h16 = (filters * H_SCALE).astype(f16).reshape(1, groups, rows, count)
    packed = jnp.concatenate([p16, h16], axis=0).transpose(1, 0, 2, 3)
    packed = packed.reshape(groups, 4 * rows, count)
    x = lax.all_to_all(packed, SEQ, split_axis=0, concat_axis=0, tiled=True).astype(f32)
    feats = conv_features(x, taps, skip, rows).reshape(2 * groups, rows, count)
    mine = lax.all_to_all(feats, ("chan",) + SEQ, split_axis=0, concat_axis=0, tiled=True)
    mine = mine.reshape(2 * slab, count)
    other = lax.ppermute(mine, "core", [(0, 1), (1, 0)])
    out_own, out_other = project(mine, other, w)
    got = lax.ppermute(out_other, "core", [(0, 1), (1, 0)])
    return jnp.where(
        core == 0,
        jnp.concatenate([out_own, got], axis=1),
        jnp.concatenate([got, out_own], axis=1),
    )


def solution(mesh):
    fine = Mesh(mesh.devices.reshape(4, 4, 4, 2, 2), SEQ + ("chan",))
    in_specs = (
        P(None, "chan", SEQ),
        P(None, "chan", None),
        P("chan", SEQ),
        P("chan"),
        P(None, "chan", SEQ),
    )
    out_specs = P(SEQ, "chan")
    return jax.shard_map(body, mesh=fine, in_specs=in_specs, out_specs=out_specs, check_vma=False)
```

time: 438 us -> 169 us (0.39); the launches traced: 429 us -> 169 us
  other arithmetic: 102 us -> 4.51 us
  matrix products: 73.5 us -> 0 us
  local copies, waits for them, and re-layouts: 59.1 us -> 10.8 us
  waiting for transfers between devices: 89.9 us -> 56.4 us
  blocking collectives: 58.3 us -> 38.8 us
  Pallas kernels: 0 us -> 18 us
  starting transfers between devices: 32.4 us -> 26.7 us
    unnamed x2 -> x0, other arithmetic: 76.2 us -> none
    dot_general x9 -> x0, matrix products: 73.5 us -> none  [the longest x1 17.6 us: body(): lax.dot_general(features, flat, (((0,), (0,)), ((), ())), preferred_eleme...]
    reduce_scatter x1 -> x0, waiting for transfers between devices: 57.3 us -> none  [body(): lax.psum_scatter(partial_out, 'chan', scatter_dimension=1, tiled=True)]
    unnamed x33 -> x14, local copies, waits for them, and re-layouts: 34.1 us -> 3.41 us
    all_to_all x2 -> x1, waiting for transfers between devices: 30.1 us -> 50.3 us  [body(): lax.all_to_all(packed, SEQ, split_axis=0, concat_axis=0, tiled=True)]
    all_to_all x2 -> x1, blocking collectives: 58.3 us -> 38.8 us  [body(): lax.all_to_all(feats, ('chan',) + SEQ, split_axis=0, concat_axis=0, tiled...]
    pallas_call x0 -> x2, Pallas kernels: none -> 18 us  [the longest x1 13.6 us: conv_features(): pl.pallas_call(lambda *refs: conv_kernel(rows, 2, *refs), out_shape=jax.S...]
    all_to_all x2 -> x1, starting transfers between devices: 28.8 us -> 11 us  [body(): lax.all_to_all(packed, SEQ, split_axis=0, concat_axis=0, tiled=True)]
  transfers between devices with their start and end apart: 5 -> 8, of which waited for: 4 -> 4; matrix products, arithmetic and copies ran while one was open for 49% -> 6% of each run, Pallas kernels for 0% -> 8%
where the time goes in v1:
time: 169 us
  waiting for transfers between devices  56.4 us (33%)
  blocking collectives  38.8 us (23%)
  starting transfers between devices  26.7 us (16%)
  Pallas kernels  18 us (11%)
  between operations  13.6 us (8%)
  local copies, waits for them, and re-layouts  10.8 us (6%)
  other arithmetic  4.51 us (3%)
    all_to_all x1, waiting for transfers between devices, body(): lax.all_to_all(packed, SEQ, split_axis=0, concat_axis=0, tiled=True)  50.3 us
    all_to_all x1, blocking collectives, body(): lax.all_to_all(feats, ('chan',) + SEQ, split_axis=0, concat_axis=0, tiled...  38.8 us
    ppermute x4, starting transfers between devices, gather_weights(): part = lax.ppermute(wt, ('z', 'core'), pairs)  13.9 us
    pallas_call x1, Pallas kernels, conv_features(): pl.pallas_call(lambda *refs: conv_kernel(rows, 2, *refs), out_shape=jax.S...  13.6 us
    all_to_all x1, starting transfers between devices, body(): lax.all_to_all(packed, SEQ, split_axis=0, concat_axis=0, tiled=True)  11 us
    pallas_call x1, Pallas kernels, project(): pl.pallas_call(proj_kernel, grid=(halves, chips // per), out_shape=(shape...  4.36 us
    dynamic_update_slice x4, local copies, waits for them, and re-layouts, gather_weights(): mine = lax.dynamic_update_slice(mine, part[None], ((z - k) % 4, 0, 0))  3.56 us
    unnamed x14, local copies, waits for them, and re-layouts  3.41 us
  transfers between devices with their start and end apart: 8, of which 4 were waited for; matrix products, arithmetic and copies ran while one was open for 6% of the time, Pallas kernels for 8%

profile of v1, /device:TPU:1, one launch (start us, length us, event | category | flops | bytes accessed | tf_op | source)
XLA Modules:
  0.0 168.8 jit_solution(2231478422106300217)
XLA Ops:
  6.5 5.2 %collective-permute-start.1 = (bf16[16,4096]{1,0:T(8,128)(2,1)}, bf16[16,4096]{1,0:T(8,128)(2,1)}, u32[]{:S(2)}, u32[]{:S(2)}) collective-permute-start(bf16[16,4096]{1,0:T(8,128)(2,1)} %bitcast.28), channel_id=1, source_target_pairs={{0,0},{2,64},{64,128},{66,192},{128,2},{130,66},{192,130},{194,194... | collective-permute-start | bytes 393224 | tf_op jit(solution)/shard_map/ppermute | solution.py:174
  11.7 3.3 %collective-permute-start.2 = (bf16[16,4096]{1,0:T(8,128)(2,1)}, bf16[16,4096]{1,0:T(8,128)(2,1)S(1)}, u32[]{:S(2)}, u32[]{:S(2)}) collective-permute-start(bf16[16,4096]{1,0:T(8,128)(2,1)} %bitcast.29), channel_id=1, source_target_pairs={{0,64},{2,128},{64,192},{66,0},{128,66},{130,130},{192,194},{194,2... | collective-permute-start | bytes 393224 | tf_op jit(solution)/shard_map/ppermute | solution.py:174
  15.0 1.5 collective-permute-start.3
  16.5 3.9 %collective-permute-start.4 = (bf16[16,4096]{1,0:T(8,128)(2,1)}, bf16[16,4096]{1,0:T(8,128)(2,1)S(1)}, u32[]{:S(2)}, u32[]{:S(2)}) collective-permute-start(bf16[16,4096]{1,0:T(8,128)(2,1)} %bitcast.31), channel_id=1, source_target_pairs={{0,192},{2,0},{64,64},{66,128},{128,194},{130,2},{192,66},{194,130... | collective-permute-start | bytes 393224 | tf_op jit(solution)/shard_map/ppermute | solution.py:174
  20.6 0.8 broadcast_in_dim.15
  21.4 1.6 bitcast_dynamic-update-slice_fusion.3
  23.0 0.7 bitcast_dynamic-update-slice_fusion.2
  23.6 0.7 bitcast_dynamic-update-slice_fusion.1
  24.3 2.2 %collective-permute-done.4 = bf16[16,4096]{1,0:T(8,128)(2,1)S(1)} collective-permute-done((bf16[16,4096]{1,0:T(8,128)(2,1)}, bf16[16,4096]{1,0:T(8,128)(2,1)S(1)}, u32[]{:S(2)}, u32[]{:S(2)}) %collective-permute-start.4) | collective-permute-done | bytes 131104 | tf_op jit(solution)/shard_map/ppermute | solution.py:174
  26.6 0.7 bitcast_dynamic-update-slice_fusion
  27.2 1.3 multiply_convert_fusion.1
  29.5 2.0 %copy.15 = f16[128,4,16,128]{3,2,1,0:T(8,128)(2,1)} copy(f16[128,4,16,128]{3,2,0,1:T(8,128)(2,1)S(1)} %maximum_bitcast_fusion) | data formatting | bytes 4194304 | tf_op jit(solution)/shard_map/transpose | solution.py:191
  31.4 11.0 %all-to-all-start = ((f16[128,64,128]{2,1,0:T(8,128)(2,1)}), f16[128,64,128]{2,1,0:T(8,128)(2,1)S(1)}, u32[]{:S(2)}, u32[]{:S(2)}) async-start(f16[128,64,128]{2,1,0:T(8,128)(2,1)} %bitcast.25), calls=%async_computation | async-start | bytes 4194304 | tf_op jit(solution)/shard_map/all_to_all | solution.py:193
  42.4 0.8 dynamic-slice_multiply_fusion
  43.4 0.8 dynamic_slice.7.refs_1_
  44.2 50.3 %all-to-all-done = f16[128,64,128]{2,1,0:T(8,128)(2,1)S(1)} async-done(((f16[128,64,128]{2,1,0:T(8,128)(2,1)}), f16[128,64,128]{2,1,0:T(8,128)(2,1)S(1)}, u32[]{:S(2)}, u32[]{:S(2)}) %all-to-all-start) | async-done | bytes 2097184 | tf_op jit(solution)/shard_map/all_to_all | solution.py:193
  95.0 13.6 %conv_features.1 = bf16[2,128,16,128]{3,2,1,0:T(8,128)(2,1)S(1)} custom-call(f32[144]{0:T(256)S(1)} %div.10.refs_0_, f32[16]{0:T(128)S(1)} %dynamic_slice.7.refs_1_, f32[8192,128]{1,0:T(8,128)S(1)} %bitcast_convert_fusion.refs_2_, bf16[256,384]{1,0:T(8,128)(2,1)S(1)} %copy-done.3, f32[128,256]{1,0:T(8,128)S(1)} %copy-done.5, bf16[768,256]{1,0:T(8,128)(2,1)S(1)} %copy-done.1, ...), custom_call_target="tpu_custom_call" | custom-call | tf_op jit(solution)/shard_map/conv_features/pallas_call | solution.py:121
  108.7 38.8 %all_to_all.10 = bf16[256,16,128]{2,1,0:T(8,128)(2,1)S(1)} all-to-all(bf16[256,16,128]{2,1,0:T(8,128)(2,1)S(1)} %bitcast.24), channel_id=1, replica_groups=mesh['z'=4,'x'=4,'y'=4,'core'=2,'chan'=2] {'chan','z','x','y','core'}, dimensions={0} | all-to-all | bytes 2097152 | tf_op jit(solution)/shard_map/all_to_all | solution.py:195
  147.5 1.3 collective-permute-start
  148.8 2.3 %collective-permute-done.other = bf16[4096,128]{1,0:T(8,128)(2,1)S(1)} collective-permute-done((bf16[4096,128]{1,0:T(8,128)(2,1)S(1)}, bf16[4096,128]{1,0:T(8,128)(2,1)S(1)}, u32[]{:S(2)}, u32[]{:S(2)}) %collective-permute-start) | collective-permute-done | bytes 1048608 | tf_op jit(solution)/shard_map/ppermute | solution.py:197
  151.1 3.4 %copy-done = bf16[16,2,32,4096]{3,2,1,0:T(8,128)(2,1)S(1)} copy-done((bf16[16,2,32,4096]{3,2,1,0:T(8,128)(2,1)S(1)}, bf16[16,2,32,4096]{3,2,1,0:T(8,128)(2,1)}, u32[]{:S(2)}) %copy-start) | copy-done | bytes 8388632
  154.5 4.4 %project.1 = (f32[128,1024]{1,0:T(8,128)S(1)}, f32[128,1024]{1,0:T(8,128)S(1)}) custom-call(bf16[4096,128]{1,0:T(8,128)(2,1)S(1)} %bitcast.23, bf16[4096,128]{1,0:T(8,128)(2,1)S(1)} %collective-permute-done.other, bf16[16,2,32,4096]{3,2,1,0:T(8,128)(2,1)S(1)} %copy-done), custom_call_target="tpu_custom_call" | custom-call | tf_op jit(solution)/shard_map/project/pallas_call | solution.py:150
  159.3 1.5 collective-permute-done.5
  160.8 1.2 maximum_select_fusion
  (25 shorter events, 2.0 us)
Async XLA Ops:
  6.5 22.0 %copy-start.6 = (f32[3,2048,128]{2,1,0:T(8,128)S(1)}, f32[3,2048,128]{2,1,0:T(8,128)}, u32[]{:S(2)}) copy-start(f32[3,2048,128]{2,1,0:T(8,128)} %param.10) | copy-start | bytes 9437188
  6.5 144.5 %all-gather.2.cloned.1.call-start = ((), (), s32[]{:S(2)}) async-start(), calls=%async_computation.2 | async-start | bytes 8912896 | tf_op jit(solution)/shard_map/all_gather | solution.py:176
  6.5 14.0 %collective-permute-start.1 = (bf16[16,4096]{1,0:T(8,128)(2,1)}, bf16[16,4096]{1,0:T(8,128)(2,1)}, u32[]{:S(2)}, u32[]{:S(2)}) collective-permute-start(bf16[16,4096]{1,0:T(8,128)(2,1)} %bitcast.28), channel_id=1, source_target_pairs={{0,0},{2,64},{64,128},{66,192},{128,2},{130,66},{192,130},{194,194... | collective-permute-start | bytes 393224 | tf_op jit(solution)/shard_map/ppermute | solution.py:174
  11.7 11.2 %collective-permute-start.2 = (bf16[16,4096]{1,0:T(8,128)(2,1)}, bf16[16,4096]{1,0:T(8,128)(2,1)S(1)}, u32[]{:S(2)}, u32[]{:S(2)}) collective-permute-start(bf16[16,4096]{1,0:T(8,128)(2,1)} %bitcast.29), channel_id=1, source_target_pairs={{0,64},{2,128},{64,192},{66,0},{128,66},{130,130},{192,194},{194,2... | collective-permute-start | bytes 393224 | tf_op jit(solution)/shard_map/ppermute | solution.py:174
  15.0 8.6 %collective-permute-start.3 = (bf16[16,4096]{1,0:T(8,128)(2,1)}, bf16[16,4096]{1,0:T(8,128)(2,1)S(1)}, u32[]{:S(2)}, u32[]{:S(2)}) collective-permute-start(bf16[16,4096]{1,0:T(8,128)(2,1)} %bitcast.30), channel_id=1, source_target_pairs={{0,128},{2,192},{64,0},{66,64},{128,130},{130,194},{192,2},{194,66... | collective-permute-start | bytes 393224 | tf_op jit(solution)/shard_map/ppermute | solution.py:174
  16.5 10.0 %collective-permute-start.4 = (bf16[16,4096]{1,0:T(8,128)(2,1)}, bf16[16,4096]{1,0:T(8,128)(2,1)S(1)}, u32[]{:S(2)}, u32[]{:S(2)}) collective-permute-start(bf16[16,4096]{1,0:T(8,128)(2,1)} %bitcast.31), channel_id=1, source_target_pairs={{0,192},{2,0},{64,64},{66,128},{128,194},{130,2},{192,66},{194,130... | collective-permute-start | bytes 393224 | tf_op jit(solution)/shard_map/ppermute | solution.py:174
  31.4 63.1 %all-to-all-start = ((f16[128,64,128]{2,1,0:T(8,128)(2,1)}), f16[128,64,128]{2,1,0:T(8,128)(2,1)S(1)}, u32[]{:S(2)}, u32[]{:S(2)}) async-start(f16[128,64,128]{2,1,0:T(8,128)(2,1)} %bitcast.25), calls=%async_computation | async-start | bytes 4194304 | tf_op jit(solution)/shard_map/all_to_all | solution.py:193
  44.2 50.8 %copy-start.1 = (bf16[768,256]{1,0:T(8,128)(2,1)S(1)}, bf16[768,256]{1,0:T(8,128)(2,1)}, u32[]{:S(2)}) copy-start(bf16[768,256]{1,0:T(8,128)(2,1)} %constant.82.clone.refs_5_) | copy-start | bytes 1179652
  44.2 50.8 %copy-start.2 = (bf16[768,256]{1,0:T(8,128)(2,1)S(1)}, bf16[768,256]{1,0:T(8,128)(2,1)}, u32[]{:S(2)}) copy-start(bf16[768,256]{1,0:T(8,128)(2,1)} %constant.83.clone.refs_6_) | copy-start | bytes 1179652
  44.2 50.8 %copy-start.3 = (bf16[256,384]{1,0:T(8,128)(2,1)S(1)}, bf16[256,384]{1,0:T(8,128)(2,1)}, u32[]{:S(2)}) copy-start(bf16[256,384]{1,0:T(8,128)(2,1)} %constant.80.clone.refs_3_) | copy-start | bytes 589828
  44.2 50.8 %copy-start.4 = (bf16[128,768]{1,0:T(8,128)(2,1)S(1)}, bf16[128,768]{1,0:T(8,128)(2,1)}, u32[]{:S(2)}) copy-start(bf16[128,768]{1,0:T(8,128)(2,1)} %constant.84.clone.refs_7_) | copy-start | bytes 589828
  44.2 50.8 %copy-start.5 = (f32[128,256]{1,0:T(8,128)S(1)}, f32[128,256]{1,0:T(8,128)}, u32[]{:S(2)}) copy-start(f32[128,256]{1,0:T(8,128)} %constant.81.clone.refs_4_) | copy-start | bytes 393220
  147.5 3.6 %collective-permute-start = (bf16[4096,128]{1,0:T(8,128)(2,1)S(1)}, bf16[4096,128]{1,0:T(8,128)(2,1)S(1)}, u32[]{:S(2)}, u32[]{:S(2)}) collective-permute-start(bf16[4096,128]{1,0:T(8,128)(2,1)S(1)} %bitcast.22), channel_id=1, source_target_pairs={{0,2},{2,0},{1,3},{3,1},{4,6},{6,4},{5,7},{7,5},{8,10},{10,8},{9,1... | collective-permute-start | bytes 3145736 | tf_op jit(solution)/shard_map/ppermute | solution.py:197
  151.1 3.4 %copy-start = (bf16[16,2,32,4096]{3,2,1,0:T(8,128)(2,1)S(1)}, bf16[16,2,32,4096]{3,2,1,0:T(8,128)(2,1)}, u32[]{:S(2)}) copy-start(bf16[16,2,32,4096]{3,2,1,0:T(8,128)(2,1)} %all-gather.2.cloned.1.call-done.w) | copy-start | bytes 25165828
  158.8 2.0 %collective-permute-start.5 = (f32[128,1024]{1,0:T(8,128)S(1)}, f32[128,1024]{1,0:T(8,128)S(1)}, u32[]{:S(2)}, u32[]{:S(2)}) collective-permute-start(f32[128,1024]{1,0:T(8,128)S(1)} %get-tuple-element.8), channel_id=1, source_target_pairs={{0,2},{2,0},{1,3},{3,1},{4,6},{6,4},{5,7},{7,5},{8,10},{10,8},{9,1... | collective-permute-start | bytes 1572872 | tf_op jit(solution)/shard_map/ppermute | solution.py:199
Sparse Core Ops, SparseCore 0:
  27.4 96.1 all-gather.1

commit v2 on v1

v2 whole, which is shorter than its diff:
```python
import math

import jax
import jax.numpy as jnp
import numpy as np
import ml_dtypes
from jax import lax
from jax.experimental import pallas as pl
from jax.experimental.pallas import tpu as pltpu
from jax.sharding import Mesh, PartitionSpec as P

BLK = 128
SEQ = ("z", "x", "y", "core")
G_SCALE = 2.0 ** 3
M_SCALE = 2.0 ** 9
H_SCALE = 2.0 ** 15
f32 = jnp.float32
bf16 = jnp.bfloat16
f16 = jnp.float16


def split_np(m):
    hi = m.astype(np.float32).astype(ml_dtypes.bfloat16)
    lo = (m - hi.astype(np.float64)).astype(np.float32).astype(ml_dtypes.bfloat16)
    return hi, lo


def tables():
    n = BLK * BLK
    k1 = np.arange(BLK)[:, None] + 0.25
    a = np.arange(BLK)[None, :]
    alpha = 2.0 * np.pi * a * k1 / BLK
    fwd_rows = np.concatenate([np.cos(alpha), np.sin(alpha)], axis=0)
    hi, lo = split_np(fwd_rows)
    rows_in = np.concatenate([hi, hi, lo], axis=1)
    tw = 2.0 * np.pi * a * k1 / n
    twiddle = np.concatenate([np.cos(tw), np.sin(tw)], axis=1).astype(np.float32)
    beta = 2.0 * np.pi * ((np.arange(BLK)[:, None] * a) % BLK) / BLK
    c, s = np.cos(beta), np.sin(beta)
    hi, lo = split_np(np.block([[c, s], [-s, c]]))
    cols_in = np.concatenate([hi, hi, lo], axis=0)
    hi, lo = split_np(np.block([[c, -s], [s, c]]))
    cols_out = np.concatenate([hi, hi, lo], axis=0)
    back = np.concatenate([np.cos(alpha).T, np.sin(alpha).T], axis=1) / (n * H_SCALE * G_SCALE * M_SCALE)
    hi, lo = split_np(back)
    rows_out = np.concatenate([hi, hi, lo], axis=1)
    return rows_in, twiddle, cols_in, cols_out, rows_out


def split(x):
    hi = x.astype(bf16)
    lo = (x - hi.astype(f32)).astype(bf16)
    return hi, lo


def dot(a, b):
    return jnp.dot(a, b, preferred_element_type=f32)


def edge_kernel(p, out):
    lane = lax.broadcasted_iota(jnp.int32, (BLK, BLK), 1)
    for q in range(0, p.shape[1], BLK):
        x = [p[i, q : q + BLK, :] for i in range(3)]
        x = [pltpu.roll(x[0], BLK - 4, 1), pltpu.roll(x[1], BLK - 2, 1), x[2]]
        t = jnp.where(lane < BLK - 4, x[0], jnp.where(lane < BLK - 2, x[1], x[2]))
        out[:, q : q + BLK] = t.T[BLK - 8 :]


def edges(projected):
    slab = projected.shape[1]
    per = slab // 4
    return pl.pallas_call(
        edge_kernel,
        grid=(4,),
        out_shape=jax.ShapeDtypeStruct((8, slab), f32),
        in_specs=[pl.BlockSpec((3, per, BLK), lambda i: (0, i, 0))],
        out_specs=pl.BlockSpec((8, per), lambda i: (0, i)),
        name="edges",
    )(projected)


def spread_table():
    e = np.zeros((32, 15, BLK), np.float32)
    for i in range(3):
        for j in range(3):
            e[8 + 8 * i + j, 3 * i + j, :] = 1.0
        e[2 * i + 3, 9 + i, 0] = 1.0
        e[2 * i + 2, 12 + i, 0] = 1.0
        e[2 * i + 3, 12 + i, 1] = 1.0
    e = e.reshape(32, 15 * BLK)
    return np.concatenate([e, e, e], axis=0).astype(ml_dtypes.bfloat16)


def gate_kernel(rows, p, halo, taps, h, table, out):
    lane = lax.broadcasted_iota(jnp.int32, (BLK, BLK), 1)
    group = BLK // rows
    left = jnp.concatenate([halo[...], taps[0], taps[1], taps[2]], axis=0)
    parts = []
    for k in range(3):
        parts.append(left.astype(bf16))
        left = left - parts[-1].astype(f32)
    cols = jnp.concatenate(parts, axis=0)
    shape = (group, rows, BLK)
    for it in range(h.shape[0] // BLK):
        sl = slice(it * BLK, (it + 1) * BLK)
        wide = lax.dot_general(
            cols[:, sl], table[...], (((0,), (0,)), ((), ())), preferred_element_type=f32
        )
        col = [wide[:, j * BLK : (j + 1) * BLK] for j in range(15)]
        mixed = []
        for i in range(3):
            x = p[i, sl, :]
            x1 = jnp.where(lane < 1, col[9 + i], pltpu.roll(x, 1, 1))
            x2 = jnp.where(lane < 2, col[12 + i], pltpu.roll(x, 2, 1))
            mixed.append(col[3 * i] * x + col[3 * i + 1] * x1 + col[3 * i + 2] * x2)
        dst = slice(it * group, (it + 1) * group)
        out[dst, 0:rows, :] = (mixed[1] * mixed[2] * G_SCALE).reshape(shape)
        out[dst, rows : 2 * rows, :] = (h[sl, :] * H_SCALE).reshape(shape)
        out[dst, 2 * rows : 3 * rows, :] = (mixed[0] * M_SCALE).reshape(shape)


def gate_pack(projected, halo, taps, filters, rows):
    slab, count = filters.shape
    steps = 8
    per = slab // steps
    table = jnp.asarray(spread_table())
    return pl.pallas_call(
        lambda *refs: gate_kernel(rows, *refs),
        grid=(steps,),
        out_shape=jax.ShapeDtypeStruct((slab // rows, 3 * rows, count), f32),
        in_specs=[
            pl.BlockSpec((3, per, count), lambda i: (0, i, 0)),
            pl.BlockSpec((8, per), lambda i: (0, i)),
            pl.BlockSpec((3, 8, per), lambda i: (0, 0, i)),
            pl.BlockSpec((per, count), lambda i: (i, 0)),
            pl.BlockSpec(table.shape, lambda i: (0, 0)),
        ],
        out_specs=pl.BlockSpec((per // rows, 3 * rows, count), lambda i: (i, 0, 0)),
        compiler_params=pltpu.CompilerParams(vmem_limit_bytes=16 * 2**20),
        name="gate_pack",
    )(projected, halo, taps, filters, table)


def conv_kernel(rows, width, skip, x, e_in, tw, c_in, c_out, e_out, out, feat):
    cos, sin = tw[:, :BLK], tw[:, BLK:]

    def load(i, c):
        return x[pl.ds(i * rows + c, BLK, stride=3 * rows), :]

    def step(it, carry):
        chans = [it * width + j for j in range(width)]
        gates = []
        pieces = []
        for c in chans:
            gate = load(0, c)
            gates.append(gate)
            pieces += [gate, load(1, c)]
        hi, lo = split(jnp.concatenate(pieces, axis=1))
        s = dot(e_in[...], jnp.concatenate([hi, lo, hi], axis=0))
        turned = []
        for j in range(2 * width):
            sr = s[:BLK, j * BLK : (j + 1) * BLK]
            si = s[BLK:, j * BLK : (j + 1) * BLK]
            turned.append(jnp.concatenate([sr * cos - si * sin, sr * sin + si * cos], axis=1))
        hi, lo = split(jnp.concatenate(turned, axis=0))
        spec = dot(jnp.concatenate([hi, lo, hi], axis=1), c_in[...])
        prods = []
        for j in range(width):
            g = spec[2 * j * BLK : (2 * j + 1) * BLK]
            h = spec[(2 * j + 1) * BLK : (2 * j + 2) * BLK]
            gr, gi, hr, hm = g[:, :BLK], g[:, BLK:], h[:, :BLK], h[:, BLK:]
            prods.append(jnp.concatenate([gr * hr - gi * hm, gr * hm + gi * hr], axis=1))
        hi, lo = split(jnp.concatenate(prods, axis=0))
        v = dot(jnp.concatenate([hi, lo, hi], axis=1), c_out[...])
        us = []
        for j in range(width):
            vr, vi = v[j * BLK : (j + 1) * BLK, :BLK], v[j * BLK : (j + 1) * BLK, BLK:]
            us.append(jnp.concatenate([vr * cos + vi * sin, vi * cos - vr * sin], axis=0))
        hi, lo = split(jnp.concatenate(us, axis=1))
        y = dot(e_out[...], jnp.concatenate([hi, lo, hi], axis=0))
        for j, c in enumerate(chans):
            f = (y[:, j * BLK : (j + 1) * BLK] + skip[c] * gates[j]) * load(2, c)
            feat[pl.ds(c, BLK, stride=rows), :] = f
        return carry

    lax.fori_loop(0, rows // width, step, 0)
    done = feat[...].reshape(BLK, rows, BLK).astype(bf16)
    out[0] = done
    out[1] = done


def conv_features(x, skip, rows):
    vmem = pl.BlockSpec(memory_space=pltpu.VMEM)
    smem = pl.BlockSpec(memory_space=pltpu.SMEM)
    consts = [jnp.asarray(t) for t in tables()]
    return pl.pallas_call(
        lambda *refs: conv_kernel(rows, 8, *refs),
        out_shape=jax.ShapeDtypeStruct((2, BLK, rows, BLK), bf16),
        in_specs=[smem] + [vmem] * 6,
        out_specs=vmem,
        scratch_shapes=[pltpu.VMEM((BLK * rows, BLK), f32)],
        compiler_params=pltpu.CompilerParams(vmem_limit_bytes=20 * 2**20),
        cost_estimate=pl.CostEstimate(flops=4 * 10**9, bytes_accessed=6 * 10**6, transcendentals=0),
        name="conv_features",
    )(skip, x.reshape(BLK * 3 * rows, BLK), *consts)


def spread(w_out):
    wt = w_out.reshape(w_out.shape[0], -1).T
    parts = []
    for k in range(4):
        pairs = []
        for zs in range(4):
            for cs in range(2):
                i = (zs % 2) * 2 + cs
                pairs.append((zs * 2 + cs, ((i + k) % 4) * 2 + zs // 2))
        parts.append(lax.ppermute(wt, ("z", "core"), pairs))
    return parts


def proj_kernel(_, own, other, wa, wb, out_own, out_other, both):
    @pl.when((pl.program_id(0) == 0) & (pl.program_id(1) == 0))
    def _():
        both[:, :BLK] = own[...]
        both[:, BLK:] = other[...]

    w = jnp.concatenate([wa[...], wb[...]], axis=1)
    t = dot(w.reshape(-1, w.shape[3]), both[...])
    out_own[...] = t[:, :BLK].T
    out_other[...] = t[:, BLK:].T


def project(pos, own, other, w):
    chips, parts, cols, depth = w.shape
    per = 8
    whole = pl.BlockSpec((depth, BLK), lambda i, j, z: (0, 0))
    out = pl.BlockSpec((BLK, per * 2 * cols), lambda i, j, z: (0, i * (chips // per) + j))
    shape = jax.ShapeDtypeStruct((BLK, chips * parts * cols), f32)

    def pick(c):
        return pl.BlockSpec(
            (per, 1, cols, depth), lambda i, j, z: (j, lax.rem(z[0] + 4 - (2 * i + c), 4), 0, 0)
        )

    return pl.pallas_call(
        proj_kernel,
        grid_spec=pltpu.PrefetchScalarGridSpec(
            num_scalar_prefetch=1,
            grid=(2, chips // per),
            in_specs=[whole, whole, pick(0), pick(1)],
            out_specs=[out, out],
            scratch_shapes=[pltpu.VMEM((depth, 2 * BLK), bf16)],
        ),
        out_shape=(shape, shape),
        compiler_params=pltpu.CompilerParams(vmem_limit_bytes=32 * 2**20),
        name="project",
    )(pos, own, other, w, w)


def body(projected, short_taps, filters, skip_gain, w_out):
    slab, count = filters.shape
    groups = lax.axis_size(SEQ)
    rows = slab // groups
    me = lax.axis_index(SEQ)
    core = lax.axis_index("core")
    skip = lax.dynamic_slice(skip_gain, (me * rows,), (rows,)) / (G_SCALE * M_SCALE)
    last = edges(projected)
    last, w_out = lax.optimization_barrier((last, w_out))
    halo = lax.ppermute(last, SEQ, [(i, i + 1) for i in range(groups - 1)])
    parts = spread(w_out)
    taps = jnp.pad(short_taps.transpose(0, 2, 1), ((0, 0), (0, 5), (0, 0)))
    packed = gate_pack(projected, halo, taps, filters, rows).astype(f16)
    packed, parts = lax.optimization_barrier((packed, parts))
    w = lax.all_gather(jnp.stack(parts), ("x", "y"))
    w = w.reshape(-1, 4, w.shape[-2], w.shape[-1])
    x = lax.all_to_all(packed, SEQ, split_axis=0, concat_axis=0, tiled=True)
    feats = conv_features(x.astype(f32), skip, rows).reshape(2 * groups, rows, count)
    mine = lax.all_to_all(feats, ("chan",) + SEQ, split_axis=0, concat_axis=0, tiled=True)
    mine = mine.reshape(2 * slab, count)
    swap = [(0, 1), (1, 0)]
    other = lax.ppermute(mine, "core", swap)
    out_own, out_other = project(lax.axis_index("z").reshape(1), mine, other, w)
    got = lax.ppermute(out_other, "core", swap)
    return jnp.where(
        core == 0,
        jnp.concatenate([out_own, got], axis=1),
        jnp.concatenate([got, out_own], axis=1),
    )


def solution(mesh):
    fine = Mesh(mesh.devices.reshape(4, 4, 4, 2, 2), SEQ + ("chan",))
    in_specs = (
        P(None, "chan", SEQ),
        P(None, "chan", None),
        P("chan", SEQ),
        P("chan"),
        P(None, "chan", SEQ),
    )
    out_specs = P(SEQ, "chan")
    return jax.shard_map(body, mesh=fine, in_specs=in_specs, out_specs=out_specs, check_vma=False)
```

time: 169 us -> 159 us (0.941)
  waiting for transfers between devices: 56.4 us -> 44.4 us
  local copies, waits for them, and re-layouts: 10.8 us -> 5.56 us
  Pallas kernels: 18 us -> 21.1 us
  starting transfers between devices: 26.7 us -> 29.8 us
    all_to_all x1, waiting for transfers between devices: 50.3 us -> 39.8 us  [body(): x = lax.all_to_all(packed, SEQ, split_axis=0, concat_axis=0, tiled=True)]
    dynamic_update_slice x4 -> x0, local copies, waits for them, and re-layouts: 3.56 us -> none  [gather_weights(): mine = lax.dynamic_update_slice(mine, part[None], ((z - k) % 4, 0, 0))]
    ppermute x6 -> x7, starting transfers between devices: 15.7 us -> 19 us  [the longest x4 13.7 us: spread(): parts.append(lax.ppermute(wt, ('z', 'core'), pairs))]
    pallas_call x2 -> x4, Pallas kernels: 18 us -> 21.1 us  [the longest x1 8.12 us: conv_features(): pl.pallas_call(lambda *refs: conv_kernel(rows, 8, *refs), out_shape=jax.S...]
    transpose x1 -> x0, local copies, waits for them, and re-layouts: 1.99 us -> none  [body(): packed = jnp.concatenate([p16, h16], axis=0).transpose(1, 0, 2, 3)]
    ppermute x6 -> x7, waiting for transfers between devices: 6.08 us -> 4.55 us  [the longest x1 2.29 us: body(): other = lax.ppermute(mine, 'core', swap)]
    unnamed x14 -> x18, local copies, waits for them, and re-layouts: 3.41 us -> 4.65 us
  transfers between devices with their start and end apart: 8 -> 9, of which waited for: 4 -> 4; matrix products, arithmetic and copies ran while one was open for 6% -> 2% of each run, Pallas kernels for 8% -> 8%
where the time goes in v2:
time: 159 us
  waiting for transfers between devices  44.4 us (28%)
  blocking collectives  39.9 us (25%)
  starting transfers between devices  29.8 us (19%)
  Pallas kernels  21.1 us (13%)
  between operations  13.6 us (9%)
  local copies, waits for them, and re-layouts  5.56 us (3%)
  other arithmetic  4.57 us (3%)
    all_to_all x1, blocking collectives, body(): lax.all_to_all(feats, ('chan',) + SEQ, split_axis=0, concat_axis=0, tiled...  39.9 us
    all_to_all x1, waiting for transfers between devices, body(): x = lax.all_to_all(packed, SEQ, split_axis=0, concat_axis=0, tiled=True)  39.8 us
    ppermute x4, starting transfers between devices, spread(): parts.append(lax.ppermute(wt, ('z', 'core'), pairs))  13.7 us
    all_to_all x1, starting transfers between devices, body(): x = lax.all_to_all(packed, SEQ, split_axis=0, concat_axis=0, tiled=True)  10.8 us
    pallas_call x1, Pallas kernels, conv_features(): pl.pallas_call(lambda *refs: conv_kernel(rows, 8, *refs), out_shape=jax.S...  8.12 us
    unnamed x18, local copies, waits for them, and re-layouts  4.65 us
    pallas_call x1, Pallas kernels, project(): pl.pallas_call(proj_kernel, grid_spec=pltpu.PrefetchScalarGridSpec(num_sc...  4.52 us
    pallas_call x1, Pallas kernels, edges(): pl.pallas_call(edge_kernel, grid=(4,), out_shape=jax.ShapeDtypeStruct((8,...  4.39 us
  transfers between devices with their start and end apart: 9, of which 4 were waited for; matrix products, arithmetic and copies ran while one was open for 2% of the time, Pallas kernels for 8%

profile of v2, /device:TPU:1, one launch (start us, length us, event | category | flops | bytes accessed | tf_op | source)
XLA Modules:
  0.0 159.0 jit_solution(1759502647561600459)
XLA Ops:
  6.5 4.4 %edges.1 = f32[8,2048]{1,0:T(8,128)} custom-call(f32[3,2048,128]{2,1,0:T(8,128)} %refs_0_.1), custom_call_target="tpu_custom_call" | custom-call | tf_op jit(solution)/shard_map/edges/pallas_call | solution.py:72
  10.9 4.9 %collective-permute-start.1 = (bf16[16,4096]{1,0:T(8,128)(2,1)}, bf16[16,4096]{1,0:T(8,128)(2,1)S(1)}, u32[]{:S(2)}, u32[]{:S(2)}) collective-permute-start(bf16[16,4096]{1,0:T(8,128)(2,1)} %bitcast.25), channel_id=1, source_target_pairs={{0,0},{2,64},{64,128},{66,192},{128,2},{130,66},{192,130},{194,194... | collective-permute-start | bytes 393224 | tf_op jit(solution)/shard_map/ppermute | solution.py:217
  15.9 3.3 %collective-permute-start.2 = (bf16[16,4096]{1,0:T(8,128)(2,1)}, bf16[16,4096]{1,0:T(8,128)(2,1)S(1)}, u32[]{:S(2)}, u32[]{:S(2)}) collective-permute-start(bf16[16,4096]{1,0:T(8,128)(2,1)} %bitcast.26), channel_id=1, source_target_pairs={{0,64},{2,128},{64,192},{66,0},{128,66},{130,130},{192,194},{194,2... | collective-permute-start | bytes 393224 | tf_op jit(solution)/shard_map/ppermute | solution.py:217
  19.1 1.4 collective-permute-start.3
  20.6 4.0 %collective-permute-start.4 = (bf16[16,4096]{1,0:T(8,128)(2,1)}, bf16[16,4096]{1,0:T(8,128)(2,1)S(1)}, u32[]{:S(2)}, u32[]{:S(2)}) collective-permute-start(bf16[16,4096]{1,0:T(8,128)(2,1)} %bitcast.28), channel_id=1, source_target_pairs={{0,192},{2,0},{64,64},{66,128},{128,194},{130,2},{192,66},{194,130... | collective-permute-start | bytes 393224 | tf_op jit(solution)/shard_map/ppermute | solution.py:217
  24.6 3.5 %collective-permute-start = (f32[8,2048]{1,0:T(8,128)}, f32[8,2048]{1,0:T(8,128)S(1)}, u32[]{:S(2)}, u32[]{:S(2)}) collective-permute-start(f32[8,2048]{1,0:T(8,128)} %edges.1), channel_id=1, source_target_pairs={{0,2},{2,4},{4,6},{6,8},{8,10},{10,12},{12,14},{14,16},{16,18},{18... | collective-permute-start | bytes 196616 | tf_op jit(solution)/shard_map/ppermute | solution.py:269
  28.2 0.9 pad.4.refs_2_
  29.1 0.7 collective-permute-done.refs_1_
  29.8 1.2 copy-done.2
  31.0 4.1 %gate_pack.1 = f32[128,48,128]{2,1,0:T(8,128)S(1)} custom-call(f32[3,2048,128]{2,1,0:T(8,128)S(1)} %copy-done.1, f32[8,2048]{1,0:T(8,128)S(1)} %collective-permute-done.refs_1_, f32[3,8,2048]{2,1,0:T(8,128)S(1)} %pad.4.refs_2_, f32[2048,128]{1,0:T(8,128)S(1)} %copy-done.2, bf16[96,1920]{1,0:T(8,128)(2,1)S(1)} %copy-done.3), custom_call_target="tpu_custom_call" | custom-call | tf_op jit(solution)/shard_map/gate_pack/pallas_call | solution.py:127
  35.1 1.4 convert_element_type.6
  36.6 0.9 pad_maximum_fusion
  37.4 10.8 %all-to-all-start = ((f16[128,48,128]{2,1,0:T(8,128)(2,1)}), f16[128,48,128]{2,1,0:T(8,128)(2,1)S(1)}, u32[]{:S(2)}, u32[]{:S(2)}) async-start(f16[128,48,128]{2,1,0:T(8,128)(2,1)} %convert_element_type.6), calls=%async_computation | async-start | bytes 3145728 | tf_op jit(solution)/shard_map/all_to_all | solution.py:276
  48.3 0.9 dynamic-slice_multiply_fusion.refs_0_
  49.2 39.8 %all-to-all-done = f16[128,48,128]{2,1,0:T(8,128)(2,1)S(1)} async-done(((f16[128,48,128]{2,1,0:T(8,128)(2,1)}), f16[128,48,128]{2,1,0:T(8,128)(2,1)S(1)}, u32[]{:S(2)}, u32[]{:S(2)}) %all-to-all-start) | async-done | bytes 1572896 | tf_op jit(solution)/shard_map/all_to_all | solution.py:276
  89.4 8.1 %conv_features.1 = bf16[2,128,16,128]{3,2,1,0:T(8,128)(2,1)S(1)} custom-call(f32[16]{0:T(128)S(1)} %dynamic-slice_multiply_fusion.refs_0_, f32[6144,128]{1,0:T(8,128)S(1)} %bitcast_convert_fusion.refs_1_, bf16[256,384]{1,0:T(8,128)(2,1)S(1)} %copy-done.6, f32[128,256]{1,0:T(8,128)S(1)} %copy-done.8, bf16[768,256]{1,0:T(8,128)(2,1)S(1)} %copy-done.4, ...), custom_call_target="tpu_custom_call" | custom-call | flops 4000000000 | bytes 6000000 | tf_op jit(solution)/shard_map/conv_features/pallas_call | solution.py:196
  97.5 39.9 %all_to_all.10 = bf16[256,16,128]{2,1,0:T(8,128)(2,1)S(1)} all-to-all(bf16[256,16,128]{2,1,0:T(8,128)(2,1)S(1)} %bitcast.19), channel_id=1, replica_groups=mesh['z'=4,'x'=4,'y'=4,'core'=2,'chan'=2] {'chan','z','x','y','core'}, dimensions={0} | all-to-all | bytes 2097152 | tf_op jit(solution)/shard_map/all_to_all | solution.py:278
  137.5 1.3 collective-permute-start.5
  138.8 2.3 %collective-permute-done.5.other = bf16[4096,128]{1,0:T(8,128)(2,1)S(1)} collective-permute-done((bf16[4096,128]{1,0:T(8,128)(2,1)S(1)}, bf16[4096,128]{1,0:T(8,128)(2,1)S(1)}, u32[]{:S(2)}, u32[]{:S(2)}) %collective-permute-start.5) | collective-permute-done | bytes 1048608 | tf_op jit(solution)/shard_map/ppermute | solution.py:281
  141.1 3.4 %copy-done = bf16[64,16,4096]{2,1,0:T(8,128)(2,1)S(1)} copy-done((bf16[64,16,4096]{2,1,0:T(8,128)(2,1)S(1)}, bf16[64,16,4096]{2,1,0:T(8,128)(2,1)}, u32[]{:S(2)}) %copy-start) | copy-done | bytes 8388632
  144.5 4.5 %project.1 = (f32[128,1024]{1,0:T(8,128)S(1)}, f32[128,1024]{1,0:T(8,128)S(1)}) custom-call(s32[1]{0:T(128)} %bitcast._, bf16[4096,128]{1,0:T(8,128)(2,1)S(1)} %bitcast.18, bf16[4096,128]{1,0:T(8,128)(2,1)S(1)} %collective-permute-done.5.other, bf16[16,4,16,4096]{3,2,1,0:T(8,128)(2,1)S(1)} %bitcast.15, bf16[16,4,16,4096]{3,2,1,0:T(8,128)(2,1)S(1)} %bitcast.16), custom_call_target="tpu_custom_call" | custom-call | tf_op jit(solution)/shard_map/project/pallas_call | solution.py:245
  149.0 0.5 collective-permute-start.6
  149.5 1.5 collective-permute-done.6
  151.0 1.1 maximum_select_fusion
  (24 shorter events, 0.4 us)
Async XLA Ops:
  6.5 23.3 %copy-start.3 = (bf16[96,1920]{1,0:T(8,128)(2,1)S(1)}, bf16[96,1920]{1,0:T(8,128)(2,1)}, u32[]{:S(2)}) copy-start(bf16[96,1920]{1,0:T(8,128)(2,1)} %constant.46.clone.refs_4_) | copy-start | bytes 1105924
  6.5 23.3 %copy-start.1 = (f32[3,2048,128]{2,1,0:T(8,128)S(1)}, f32[3,2048,128]{2,1,0:T(8,128)}, u32[]{:S(2)}) copy-start(f32[3,2048,128]{2,1,0:T(8,128)} %refs_0_.1) | copy-start | bytes 9437188
  6.5 134.6 %all-gather.3.cloned.1.call-start = ((), (), s32[]{:S(2)}) async-start(), calls=%async_computation.2 | async-start | bytes 8912896 | tf_op jit(solution)/shard_map/all_gather | solution.py:274
  10.9 25.6 %collective-permute-start.1 = (bf16[16,4096]{1,0:T(8,128)(2,1)}, bf16[16,4096]{1,0:T(8,128)(2,1)S(1)}, u32[]{:S(2)}, u32[]{:S(2)}) collective-permute-start(bf16[16,4096]{1,0:T(8,128)(2,1)} %bitcast.25), channel_id=1, source_target_pairs={{0,0},{2,64},{64,128},{66,192},{128,2},{130,66},{192,130},{194,194... | collective-permute-start | bytes 393224 | tf_op jit(solution)/shard_map/ppermute | solution.py:217
  15.9 20.7 %collective-permute-start.2 = (bf16[16,4096]{1,0:T(8,128)(2,1)}, bf16[16,4096]{1,0:T(8,128)(2,1)S(1)}, u32[]{:S(2)}, u32[]{:S(2)}) collective-permute-start(bf16[16,4096]{1,0:T(8,128)(2,1)} %bitcast.26), channel_id=1, source_target_pairs={{0,64},{2,128},{64,192},{66,0},{128,66},{130,130},{192,194},{194,2... | collective-permute-start | bytes 393224 | tf_op jit(solution)/shard_map/ppermute | solution.py:217
  19.1 17.4 %collective-permute-start.3 = (bf16[16,4096]{1,0:T(8,128)(2,1)}, bf16[16,4096]{1,0:T(8,128)(2,1)S(1)}, u32[]{:S(2)}, u32[]{:S(2)}) collective-permute-start(bf16[16,4096]{1,0:T(8,128)(2,1)} %bitcast.27), channel_id=1, source_target_pairs={{0,128},{2,192},{64,0},{66,64},{128,130},{130,194},{192,2},{194,66... | collective-permute-start | bytes 393224 | tf_op jit(solution)/shard_map/ppermute | solution.py:217
  20.6 16.0 %collective-permute-start.4 = (bf16[16,4096]{1,0:T(8,128)(2,1)}, bf16[16,4096]{1,0:T(8,128)(2,1)S(1)}, u32[]{:S(2)}, u32[]{:S(2)}) collective-permute-start(bf16[16,4096]{1,0:T(8,128)(2,1)} %bitcast.28), channel_id=1, source_target_pairs={{0,192},{2,0},{64,64},{66,128},{128,194},{130,2},{192,66},{194,130... | collective-permute-start | bytes 393224 | tf_op jit(solution)/shard_map/ppermute | solution.py:217
  24.6 5.2 %collective-permute-start = (f32[8,2048]{1,0:T(8,128)}, f32[8,2048]{1,0:T(8,128)S(1)}, u32[]{:S(2)}, u32[]{:S(2)}) collective-permute-start(f32[8,2048]{1,0:T(8,128)} %edges.1), channel_id=1, source_target_pairs={{0,2},{2,4},{4,6},{6,8},{8,10},{10,12},{12,14},{14,16},{16,18},{18... | collective-permute-start | bytes 196616 | tf_op jit(solution)/shard_map/ppermute | solution.py:269
  29.8 1.2 copy-start.2
  37.4 51.6 %all-to-all-start = ((f16[128,48,128]{2,1,0:T(8,128)(2,1)}), f16[128,48,128]{2,1,0:T(8,128)(2,1)S(1)}, u32[]{:S(2)}, u32[]{:S(2)}) async-start(f16[128,48,128]{2,1,0:T(8,128)(2,1)} %convert_element_type.6), calls=%async_computation | async-start | bytes 3145728 | tf_op jit(solution)/shard_map/all_to_all | solution.py:276
  48.3 41.1 %copy-start.4 = (bf16[768,256]{1,0:T(8,128)(2,1)S(1)}, bf16[768,256]{1,0:T(8,128)(2,1)}, u32[]{:S(2)}) copy-start(bf16[768,256]{1,0:T(8,128)(2,1)} %constant.49.clone.refs_4_) | copy-start | bytes 1179652
  48.3 41.1 %copy-start.5 = (bf16[768,256]{1,0:T(8,128)(2,1)S(1)}, bf16[768,256]{1,0:T(8,128)(2,1)}, u32[]{:S(2)}) copy-start(bf16[768,256]{1,0:T(8,128)(2,1)} %constant.50.clone.refs_5_) | copy-start | bytes 1179652
  48.3 41.1 %copy-start.6 = (bf16[256,384]{1,0:T(8,128)(2,1)S(1)}, bf16[256,384]{1,0:T(8,128)(2,1)}, u32[]{:S(2)}) copy-start(bf16[256,384]{1,0:T(8,128)(2,1)} %constant.47.clone.refs_2_) | copy-start | bytes 589828
  48.3 41.1 %copy-start.7 = (bf16[128,768]{1,0:T(8,128)(2,1)S(1)}, bf16[128,768]{1,0:T(8,128)(2,1)}, u32[]{:S(2)}) copy-start(bf16[128,768]{1,0:T(8,128)(2,1)} %constant.51.clone.refs_6_) | copy-start | bytes 589828
  48.3 41.1 %copy-start.8 = (f32[128,256]{1,0:T(8,128)S(1)}, f32[128,256]{1,0:T(8,128)}, u32[]{:S(2)}) copy-start(f32[128,256]{1,0:T(8,128)} %constant.48.clone.refs_3_) | copy-start | bytes 393220
  137.5 3.6 %collective-permute-start.5 = (bf16[4096,128]{1,0:T(8,128)(2,1)S(1)}, bf16[4096,128]{1,0:T(8,128)(2,1)S(1)}, u32[]{:S(2)}, u32[]{:S(2)}) collective-permute-start(bf16[4096,128]{1,0:T(8,128)(2,1)S(1)} %bitcast.17), channel_id=1, source_target_pairs={{0,2},{2,0},{1,3},{3,1},{4,6},{6,4},{5,7},{7,5},{8,10},{10,8},{9,1... | collective-permute-start | bytes 3145736 | tf_op jit(solution)/shard_map/ppermute | solution.py:281
  141.1 3.4 %copy-start = (bf16[64,16,4096]{2,1,0:T(8,128)(2,1)S(1)}, bf16[64,16,4096]{2,1,0:T(8,128)(2,1)}, u32[]{:S(2)}) copy-start(bf16[64,16,4096]{2,1,0:T(8,128)(2,1)} %all-gather.3.cloned.1.call-done) | copy-start | bytes 25165828
  149.0 2.0 %collective-permute-start.6 = (f32[128,1024]{1,0:T(8,128)S(1)}, f32[128,1024]{1,0:T(8,128)S(1)}, u32[]{:S(2)}, u32[]{:S(2)}) collective-permute-start(f32[128,1024]{1,0:T(8,128)S(1)} %get-tuple-element.22), channel_id=1, source_target_pairs={{0,2},{2,0},{1,3},{3,1},{4,6},{6,4},{5,7},{7,5},{8,10},{10,8},{9,1... | collective-permute-start | bytes 1572872 | tf_op jit(solution)/shard_map/ppermute | solution.py:283
Sparse Core Ops, SparseCore 0:
  37.6 97.1 all-gather.2

commit v3 on v2

--- a/solution.py
+++ b/solution.py
@@ -67,14 +67,12 @@
 
 
 def edges(projected):
-    slab = projected.shape[1]
-    per = slab // 4
+    vmem = pl.BlockSpec(memory_space=pltpu.VMEM)
     return pl.pallas_call(
         edge_kernel,
-        grid=(4,),
-        out_shape=jax.ShapeDtypeStruct((8, slab), f32),
-        in_specs=[pl.BlockSpec((3, per, BLK), lambda i: (0, i, 0))],
-        out_specs=pl.BlockSpec((8, per), lambda i: (0, i)),
+        out_shape=jax.ShapeDtypeStruct((8, projected.shape[1]), f32),
+        in_specs=[vmem],
+        out_specs=vmem,
         name="edges",
     )(projected)
 
@@ -91,10 +89,14 @@
     return np.concatenate([e, e, e], axis=0).astype(ml_dtypes.bfloat16)
 
 
-def gate_kernel(rows, p, halo, taps, h, table, out):
+def gate_kernel(rows, p, halo, taps, h, table, out, left_ref):
     lane = lax.broadcasted_iota(jnp.int32, (BLK, BLK), 1)
     group = BLK // rows
-    left = jnp.concatenate([halo[...], taps[0], taps[1], taps[2]], axis=0)
+    left_ref[0:8, :] = halo[...]
+    left_ref[8:32, :] = jnp.zeros((24, left_ref.shape[1]), f32)
+    for i in range(3):
+        left_ref[8 + 8 * i : 11 + 8 * i, :] = taps[i]
+    left = left_ref[...]
     parts = []
     for k in range(3):
         parts.append(left.astype(bf16))
@@ -121,24 +123,17 @@
 
 def gate_pack(projected, halo, taps, filters, rows):
     slab, count = filters.shape
-    steps = 8
-    per = slab // steps
-    table = jnp.asarray(spread_table())
+    vmem = pl.BlockSpec(memory_space=pltpu.VMEM)
     return pl.pallas_call(
         lambda *refs: gate_kernel(rows, *refs),
-        grid=(steps,),
         out_shape=jax.ShapeDtypeStruct((slab // rows, 3 * rows, count), f32),
-        in_specs=[
-            pl.BlockSpec((3, per, count), lambda i: (0, i, 0)),
-            pl.BlockSpec((8, per), lambda i: (0, i)),
-            pl.BlockSpec((3, 8, per), lambda i: (0, 0, i)),
-            pl.BlockSpec((per, count), lambda i: (i, 0)),
-            pl.BlockSpec(table.shape, lambda i: (0, 0)),
-        ],
-        out_specs=pl.BlockSpec((per // rows, 3 * rows, count), lambda i: (i, 0, 0)),
+        in_specs=[vmem] * 5,
+        out_specs=vmem,
+        scratch_shapes=[pltpu.VMEM((32, slab), f32)],
         compiler_params=pltpu.CompilerParams(vmem_limit_bytes=16 * 2**20),
+        cost_estimate=pl.CostEstimate(flops=10**9, bytes_accessed=8 * 10**6, transcendentals=0),
         name="gate_pack",
-    )(projected, halo, taps, filters, table)
+    )(projected, halo, taps, filters, jnp.asarray(spread_table()))
 
 
 def conv_kernel(rows, width, skip, x, e_in, tw, c_in, c_out, e_out, out, feat):
@@ -268,7 +263,7 @@
     last, w_out = lax.optimization_barrier((last, w_out))
     halo = lax.ppermute(last, SEQ, [(i, i + 1) for i in range(groups - 1)])
     parts = spread(w_out)
-    taps = jnp.pad(short_taps.transpose(0, 2, 1), ((0, 0), (0, 5), (0, 0)))
+    taps = short_taps.transpose(0, 2, 1)
     packed = gate_pack(projected, halo, taps, filters, rows).astype(f16)
     packed, parts = lax.optimization_barrier((packed, parts))
     w = lax.all_gather(jnp.stack(parts), ("x", "y"))
@@ -277,6 +272,7 @@
     feats = conv_features(x.astype(f32), skip, rows).reshape(2 * groups, rows, count)
     mine = lax.all_to_all(feats, ("chan",) + SEQ, split_axis=0, concat_axis=0, tiled=True)
     mine = mine.reshape(2 * slab, count)
+    mine, w = lax.optimization_barrier((mine, w))
     swap = [(0, 1), (1, 0)]
     other = lax.ppermute(mine, "core", swap)
     out_own, out_other = project(lax.axis_index("z").reshape(1), mine, other, w)

time: 159 us -> 156 us (0.981)
  Pallas kernels: 21.1 us -> 18.6 us
  starting transfers between devices: 29.8 us -> 27.5 us
    ppermute x4, starting transfers between devices: 13.7 us -> 11 us  [spread(): parts.append(lax.ppermute(wt, ('z', 'core'), pairs))]
    pallas_call x2, Pallas kernels: 8.47 us -> 5.98 us  [the longest x1 3.62 us: edges(): pl.pallas_call(edge_kernel, out_shape=jax.ShapeDtypeStruct((8, projected....]
    unnamed x18 -> x20, local copies, waits for them, and re-layouts: 4.65 us -> 6.52 us
  transfers between devices with their start and end apart: 9 -> 9, of which waited for: 4 -> 3; matrix products, arithmetic and copies ran while one was open for 2% -> 2% of each run, Pallas kernels for 8% -> 7%
where the time goes in v3:
time: 156 us; the launch traced here: 155 us
  waiting for transfers between devices  43.7 us (28%)
  blocking collectives  41 us (26%)
  starting transfers between devices  27.5 us (18%)
  Pallas kernels  18.6 us (12%)
  between operations  13.6 us (9%)
  local copies, waits for them, and re-layouts  6.52 us (4%)
  other arithmetic  4.55 us (3%)
    all_to_all x1, blocking collectives, body(): lax.all_to_all(feats, ('chan',) + SEQ, split_axis=0, concat_axis=0, tiled...  41 us
    all_to_all x1, waiting for transfers between devices, body(): x = lax.all_to_all(packed, SEQ, split_axis=0, concat_axis=0, tiled=True)  39.8 us
    ppermute x4, starting transfers between devices, spread(): parts.append(lax.ppermute(wt, ('z', 'core'), pairs))  11 us
    all_to_all x1, starting transfers between devices, body(): x = lax.all_to_all(packed, SEQ, split_axis=0, concat_axis=0, tiled=True)  10.1 us
    pallas_call x1, Pallas kernels, conv_features(): pl.pallas_call(lambda *refs: conv_kernel(rows, 8, *refs), out_shape=jax.S...  8.12 us
    unnamed x20, local copies, waits for them, and re-layouts  6.52 us
    ppermute x1, starting transfers between devices, body(): halo = lax.ppermute(last, SEQ, [(i, i + 1) for i in range(groups - 1)])  4.58 us
    pallas_call x1, Pallas kernels, project(): pl.pallas_call(proj_kernel, grid_spec=pltpu.PrefetchScalarGridSpec(num_sc...  4.52 us
  transfers between devices with their start and end apart: 9, of which 3 were waited for; matrix products, arithmetic and copies ran while one was open for 2% of the time, Pallas kernels for 7%

profile of v3, /device:TPU:1, one launch (start us, length us, event | category | flops | bytes accessed | tf_op | source)
XLA Modules:
  0.0 155.5 jit_solution(8934120877810972724)
XLA Ops:
  6.5 3.6 %edges.1 = f32[8,2048]{1,0:T(8,128)} custom-call(f32[3,2048,128]{2,1,0:T(8,128)} %refs_0_.1), custom_call_target="tpu_custom_call" | custom-call | tf_op jit(solution)/shard_map/edges/pallas_call | solution.py:71
  10.2 4.6 %collective-permute-start = (f32[8,2048]{1,0:T(8,128)}, f32[8,2048]{1,0:T(8,128)S(1)}, u32[]{:S(2)}, u32[]{:S(2)}) collective-permute-start(f32[8,2048]{1,0:T(8,128)} %edges.1), channel_id=1, source_target_pairs={{0,2},{2,4},{4,6},{6,8},{8,10},{10,12},{12,14},{14,16},{16,18},{18... | collective-permute-start | bytes 196616 | tf_op jit(solution)/shard_map/ppermute | solution.py:264
  14.8 2.3 %collective-permute-start.1 = (bf16[16,4096]{1,0:T(8,128)(2,1)}, bf16[16,4096]{1,0:T(8,128)(2,1)S(1)}, u32[]{:S(2)}, u32[]{:S(2)}) collective-permute-start(bf16[16,4096]{1,0:T(8,128)(2,1)} %bitcast.25), channel_id=1, source_target_pairs={{0,0},{2,64},{64,128},{66,192},{128,2},{130,66},{192,130},{194,194... | collective-permute-start | bytes 393224 | tf_op jit(solution)/shard_map/ppermute | solution.py:212
  17.0 4.2 %collective-permute-start.2 = (bf16[16,4096]{1,0:T(8,128)(2,1)}, bf16[16,4096]{1,0:T(8,128)(2,1)S(1)}, u32[]{:S(2)}, u32[]{:S(2)}) collective-permute-start(bf16[16,4096]{1,0:T(8,128)(2,1)} %bitcast.26), channel_id=1, source_target_pairs={{0,64},{2,128},{64,192},{66,0},{128,66},{130,130},{192,194},{194,2... | collective-permute-start | bytes 393224 | tf_op jit(solution)/shard_map/ppermute | solution.py:212
  21.2 1.9 %collective-permute-start.3 = (bf16[16,4096]{1,0:T(8,128)(2,1)}, bf16[16,4096]{1,0:T(8,128)(2,1)S(1)}, u32[]{:S(2)}, u32[]{:S(2)}) collective-permute-start(bf16[16,4096]{1,0:T(8,128)(2,1)} %bitcast.27), channel_id=1, source_target_pairs={{0,128},{2,192},{64,0},{66,64},{128,130},{130,194},{192,2},{194,66... | collective-permute-start | bytes 393224 | tf_op jit(solution)/shard_map/ppermute | solution.py:212
  23.1 2.6 %collective-permute-start.4 = (bf16[16,4096]{1,0:T(8,128)(2,1)}, bf16[16,4096]{1,0:T(8,128)(2,1)S(1)}, u32[]{:S(2)}, u32[]{:S(2)}) collective-permute-start(bf16[16,4096]{1,0:T(8,128)(2,1)} %bitcast.28), channel_id=1, source_target_pairs={{0,192},{2,0},{64,64},{66,128},{128,194},{130,2},{192,66},{194,130... | collective-permute-start | bytes 393224 | tf_op jit(solution)/shard_map/ppermute | solution.py:212
  25.8 1.2 copy-done.2
  27.0 1.0 copy-done.3
  28.0 0.9 copy-done.4
  28.9 2.4 %gate_pack.1 = f32[128,48,128]{2,1,0:T(8,128)S(1)} custom-call(f32[3,2048,128]{2,1,0:T(8,128)S(1)} %copy-done.1, f32[8,2048]{1,0:T(8,128)S(1)} %collective-permute-done.refs_1_, f32[3,3,2048]{2,1,0:T(4,128)S(1)} %bitcast.20, f32[2048,128]{1,0:T(8,128)S(1)} %copy-done.2, bf16[96,1920]{1,0:T(8,128)(2,1)S(1)} %copy-done.3), custom_call_target="tpu_custom_call" | custom-call | flops 1000000000 | bytes 8000000 | tf_op jit(solution)/shard_map/gate_pack/pallas_call | solution.py:127
  31.3 1.4 convert_element_type.4
  32.7 0.9 pad_maximum_fusion
  33.6 10.1 %all-to-all-start = ((f16[128,48,128]{2,1,0:T(8,128)(2,1)}), f16[128,48,128]{2,1,0:T(8,128)(2,1)S(1)}, u32[]{:S(2)}, u32[]{:S(2)}) async-start(f16[128,48,128]{2,1,0:T(8,128)(2,1)} %convert_element_type.4), calls=%async_computation | async-start | bytes 3145728 | tf_op jit(solution)/shard_map/all_to_all | solution.py:271
  43.8 0.9 dynamic-slice_multiply_fusion.refs_0_
  44.6 39.8 %all-to-all-done = f16[128,48,128]{2,1,0:T(8,128)(2,1)S(1)} async-done(((f16[128,48,128]{2,1,0:T(8,128)(2,1)}), f16[128,48,128]{2,1,0:T(8,128)(2,1)S(1)}, u32[]{:S(2)}, u32[]{:S(2)}) %all-to-all-start) | async-done | bytes 1572896 | tf_op jit(solution)/shard_map/all_to_all | solution.py:271
  84.9 8.1 %conv_features.1 = bf16[2,128,16,128]{3,2,1,0:T(8,128)(2,1)S(1)} custom-call(f32[16]{0:T(128)S(1)} %dynamic-slice_multiply_fusion.refs_0_, f32[6144,128]{1,0:T(8,128)S(1)} %bitcast_convert_fusion.refs_1_, bf16[256,384]{1,0:T(8,128)(2,1)S(1)} %copy-done.7, f32[128,256]{1,0:T(8,128)S(1)} %copy-done.9, bf16[768,256]{1,0:T(8,128)(2,1)S(1)} %copy-done.5, ...), custom_call_target="tpu_custom_call" | custom-call | flops 4000000000 | bytes 6000000 | tf_op jit(solution)/shard_map/conv_features/pallas_call | solution.py:191
  93.0 41.0 %all_to_all.10 = bf16[256,16,128]{2,1,0:T(8,128)(2,1)S(1)} all-to-all(bf16[256,16,128]{2,1,0:T(8,128)(2,1)S(1)} %bitcast.19), channel_id=1, replica_groups=mesh['z'=4,'x'=4,'y'=4,'core'=2,'chan'=2] {'chan','z','x','y','core'}, dimensions={0} | all-to-all | bytes 2097152 | tf_op jit(solution)/shard_map/all_to_all | solution.py:273
  134.0 1.3 collective-permute-start.5
  135.3 2.3 %collective-permute-done.5.other = bf16[4096,128]{1,0:T(8,128)(2,1)S(1)} collective-permute-done((bf16[4096,128]{1,0:T(8,128)(2,1)S(1)}, bf16[4096,128]{1,0:T(8,128)(2,1)S(1)}, u32[]{:S(2)}, u32[]{:S(2)}) %collective-permute-start.5) | collective-permute-done | bytes 1048608 | tf_op jit(solution)/shard_map/ppermute | solution.py:277
  137.6 3.4 %copy-done = bf16[64,16,4096]{2,1,0:T(8,128)(2,1)S(1)} copy-done((bf16[64,16,4096]{2,1,0:T(8,128)(2,1)S(1)}, bf16[64,16,4096]{2,1,0:T(8,128)(2,1)}, u32[]{:S(2)}) %copy-start) | copy-done | bytes 8388632
  141.0 4.5 %project.1 = (f32[128,1024]{1,0:T(8,128)S(1)}, f32[128,1024]{1,0:T(8,128)S(1)}) custom-call(s32[1]{0:T(128)} %bitcast._, bf16[4096,128]{1,0:T(8,128)(2,1)S(1)} %bitcast.18, bf16[4096,128]{1,0:T(8,128)(2,1)S(1)} %collective-permute-done.5.other, bf16[16,4,16,4096]{3,2,1,0:T(8,128)(2,1)S(1)} %bitcast.15, bf16[16,4,16,4096]{3,2,1,0:T(8,128)(2,1)S(1)} %bitcast.16), custom_call_target="tpu_custom_call" | custom-call | tf_op jit(solution)/shard_map/project/pallas_call | solution.py:240
  145.5 0.5 collective-permute-start.6
  146.0 1.5 collective-permute-done.6
  147.5 1.1 maximum_select_fusion
  (25 shorter events, 0.4 us)
Async XLA Ops:
  6.5 19.3 %copy-start.1 = (f32[3,2048,128]{2,1,0:T(8,128)S(1)}, f32[3,2048,128]{2,1,0:T(8,128)}, u32[]{:S(2)}) copy-start(f32[3,2048,128]{2,1,0:T(8,128)} %refs_0_.1) | copy-start | bytes 9437188
  6.5 127.5 %all-gather.3.cloned.1.call-start = ((), (), s32[]{:S(2)}) async-start(), calls=%async_computation.2 | async-start | bytes 8912896 | tf_op jit(solution)/shard_map/all_gather | solution.py:269
  10.2 15.6 %collective-permute-start = (f32[8,2048]{1,0:T(8,128)}, f32[8,2048]{1,0:T(8,128)S(1)}, u32[]{:S(2)}, u32[]{:S(2)}) collective-permute-start(f32[8,2048]{1,0:T(8,128)} %edges.1), channel_id=1, source_target_pairs={{0,2},{2,4},{4,6},{6,8},{8,10},{10,12},{12,14},{14,16},{16,18},{18... | collective-permute-start | bytes 196616 | tf_op jit(solution)/shard_map/ppermute | solution.py:264
  14.8 17.9 %collective-permute-start.1 = (bf16[16,4096]{1,0:T(8,128)(2,1)}, bf16[16,4096]{1,0:T(8,128)(2,1)S(1)}, u32[]{:S(2)}, u32[]{:S(2)}) collective-permute-start(bf16[16,4096]{1,0:T(8,128)(2,1)} %bitcast.25), channel_id=1, source_target_pairs={{0,0},{2,64},{64,128},{66,192},{128,2},{130,66},{192,130},{194,194... | collective-permute-start | bytes 393224 | tf_op jit(solution)/shard_map/ppermute | solution.py:212
  17.0 15.7 %collective-permute-start.2 = (bf16[16,4096]{1,0:T(8,128)(2,1)}, bf16[16,4096]{1,0:T(8,128)(2,1)S(1)}, u32[]{:S(2)}, u32[]{:S(2)}) collective-permute-start(bf16[16,4096]{1,0:T(8,128)(2,1)} %bitcast.26), channel_id=1, source_target_pairs={{0,64},{2,128},{64,192},{66,0},{128,66},{130,130},{192,194},{194,2... | collective-permute-start | bytes 393224 | tf_op jit(solution)/shard_map/ppermute | solution.py:212
  21.2 11.5 %collective-permute-start.3 = (bf16[16,4096]{1,0:T(8,128)(2,1)}, bf16[16,4096]{1,0:T(8,128)(2,1)S(1)}, u32[]{:S(2)}, u32[]{:S(2)}) collective-permute-start(bf16[16,4096]{1,0:T(8,128)(2,1)} %bitcast.27), channel_id=1, source_target_pairs={{0,128},{2,192},{64,0},{66,64},{128,130},{130,194},{192,2},{194,66... | collective-permute-start | bytes 393224 | tf_op jit(solution)/shard_map/ppermute | solution.py:212
  23.1 9.6 %collective-permute-start.4 = (bf16[16,4096]{1,0:T(8,128)(2,1)}, bf16[16,4096]{1,0:T(8,128)(2,1)S(1)}, u32[]{:S(2)}, u32[]{:S(2)}) collective-permute-start(bf16[16,4096]{1,0:T(8,128)(2,1)} %bitcast.28), channel_id=1, source_target_pairs={{0,192},{2,0},{64,64},{66,128},{128,194},{130,2},{192,66},{194,130... | collective-permute-start | bytes 393224 | tf_op jit(solution)/shard_map/ppermute | solution.py:212
  25.8 1.2 copy-start.2
  27.0 1.0 copy-start.3
  28.0 0.9 copy-start.4
  33.6 50.9 %all-to-all-start = ((f16[128,48,128]{2,1,0:T(8,128)(2,1)}), f16[128,48,128]{2,1,0:T(8,128)(2,1)S(1)}, u32[]{:S(2)}, u32[]{:S(2)}) async-start(f16[128,48,128]{2,1,0:T(8,128)(2,1)} %convert_element_type.4), calls=%async_computation | async-start | bytes 3145728 | tf_op jit(solution)/shard_map/all_to_all | solution.py:271
  43.7 41.1 %copy-start.5 = (bf16[768,256]{1,0:T(8,128)(2,1)S(1)}, bf16[768,256]{1,0:T(8,128)(2,1)}, u32[]{:S(2)}) copy-start(bf16[768,256]{1,0:T(8,128)(2,1)} %constant.47.clone.refs_4_) | copy-start | bytes 1179652
  43.7 41.1 %copy-start.6 = (bf16[768,256]{1,0:T(8,128)(2,1)S(1)}, bf16[768,256]{1,0:T(8,128)(2,1)}, u32[]{:S(2)}) copy-start(bf16[768,256]{1,0:T(8,128)(2,1)} %constant.48.clone.refs_5_) | copy-start | bytes 1179652
  43.7 41.1 %copy-start.7 = (bf16[256,384]{1,0:T(8,128)(2,1)S(1)}, bf16[256,384]{1,0:T(8,128)(2,1)}, u32[]{:S(2)}) copy-start(bf16[256,384]{1,0:T(8,128)(2,1)} %constant.45.clone.refs_2_) | copy-start | bytes 589828
  43.8 41.1 %copy-start.8 = (bf16[128,768]{1,0:T(8,128)(2,1)S(1)}, bf16[128,768]{1,0:T(8,128)(2,1)}, u32[]{:S(2)}) copy-start(bf16[128,768]{1,0:T(8,128)(2,1)} %constant.49.clone.refs_6_) | copy-start | bytes 589828
  43.8 41.1 %copy-start.9 = (f32[128,256]{1,0:T(8,128)S(1)}, f32[128,256]{1,0:T(8,128)}, u32[]{:S(2)}) copy-start(f32[128,256]{1,0:T(8,128)} %constant.46.clone.refs_3_) | copy-start | bytes 393220
  134.0 3.6 %collective-permute-start.5 = (bf16[4096,128]{1,0:T(8,128)(2,1)S(1)}, bf16[4096,128]{1,0:T(8,128)(2,1)S(1)}, u32[]{:S(2)}, u32[]{:S(2)}) collective-permute-start(bf16[4096,128]{1,0:T(8,128)(2,1)S(1)} %bitcast.17), channel_id=1, source_target_pairs={{0,2},{2,0},{1,3},{3,1},{4,6},{6,4},{5,7},{7,5},{8,10},{10,8},{9,1... | collective-permute-start | bytes 3145736 | tf_op jit(solution)/shard_map/ppermute | solution.py:277
  137.6 3.4 %copy-start = (bf16[64,16,4096]{2,1,0:T(8,128)(2,1)S(1)}, bf16[64,16,4096]{2,1,0:T(8,128)(2,1)}, u32[]{:S(2)}) copy-start(bf16[64,16,4096]{2,1,0:T(8,128)(2,1)} %all-gather.3.cloned.1.call-done) | copy-start | bytes 25165828
  145.5 2.0 %collective-permute-start.6 = (f32[128,1024]{1,0:T(8,128)S(1)}, f32[128,1024]{1,0:T(8,128)S(1)}, u32[]{:S(2)}, u32[]{:S(2)}) collective-permute-start(f32[128,1024]{1,0:T(8,128)S(1)} %get-tuple-element.26), channel_id=1, source_target_pairs={{0,2},{2,0},{1,3},{3,1},{4,6},{6,4},{5,7},{7,5},{8,10},{10,8},{9,1... | collective-permute-start | bytes 1572872 | tf_op jit(solution)/shard_map/ppermute | solution.py:279
Sparse Core Ops, SparseCore 0:
  33.7 97.7 all-gather.2

commit v4 on v3

--- a/solution.py
+++ b/solution.py
@@ -213,43 +213,32 @@
     return parts
 
 
-def proj_kernel(_, own, other, wa, wb, out_own, out_other, both):
-    @pl.when((pl.program_id(0) == 0) & (pl.program_id(1) == 0))
-    def _():
-        both[:, :BLK] = own[...]
-        both[:, BLK:] = other[...]
-
-    w = jnp.concatenate([wa[...], wb[...]], axis=1)
-    t = dot(w.reshape(-1, w.shape[3]), both[...])
-    out_own[...] = t[:, :BLK].T
-    out_other[...] = t[:, BLK:].T
+def proj_kernel(pos, own, other, w, out_own, out_other, acc):
+    chips, parts, cols, depth = w.shape
+    both = jnp.concatenate([own[...], other[...]], axis=1)
+    for i in range(parts):
+        k = lax.rem(pos[0] + 4 - i, 4)
+        t = dot(w[:, k].reshape(chips * cols, depth), both)
+        acc[i // 2, :, i % 2] = t.reshape(chips, cols, 2 * BLK)
+    flat = acc[...].reshape(chips * parts * cols, 2 * BLK)
+    for c in range(0, flat.shape[0], BLK):
+        out_own[:, c : c + BLK] = flat[c : c + BLK, :BLK].T
+        out_other[:, c : c + BLK] = flat[c : c + BLK, BLK:].T
 
 
 def project(pos, own, other, w):
+    vmem = pl.BlockSpec(memory_space=pltpu.VMEM)
     chips, parts, cols, depth = w.shape
-    per = 8
-    whole = pl.BlockSpec((depth, BLK), lambda i, j, z: (0, 0))
-    out = pl.BlockSpec((BLK, per * 2 * cols), lambda i, j, z: (0, i * (chips // per) + j))
     shape = jax.ShapeDtypeStruct((BLK, chips * parts * cols), f32)
-
-    def pick(c):
-        return pl.BlockSpec(
-            (per, 1, cols, depth), lambda i, j, z: (j, lax.rem(z[0] + 4 - (2 * i + c), 4), 0, 0)
-        )
-
     return pl.pallas_call(
         proj_kernel,
-        grid_spec=pltpu.PrefetchScalarGridSpec(
-            num_scalar_prefetch=1,
-            grid=(2, chips // per),
-            in_specs=[whole, whole, pick(0), pick(1)],
-            out_specs=[out, out],
-            scratch_shapes=[pltpu.VMEM((depth, 2 * BLK), bf16)],
-        ),
         out_shape=(shape, shape),
-        compiler_params=pltpu.CompilerParams(vmem_limit_bytes=32 * 2**20),
+        in_specs=[pl.BlockSpec(memory_space=pltpu.SMEM), vmem, vmem, vmem],
+        out_specs=(vmem, vmem),
+        scratch_shapes=[pltpu.VMEM((2, chips, 2, cols, 2 * BLK), f32)],
+        compiler_params=pltpu.CompilerParams(vmem_limit_bytes=24 * 2**20),
         name="project",
-    )(pos, own, other, w, w)
+    )(pos, own, other, w)
 
 
 def body(projected, short_taps, filters, skip_gain, w_out):

time: 156 us -> 154 us (0.987)
  Pallas kernels: 18.6 us -> 16.5 us
    pallas_call x1, Pallas kernels: 4.52 us -> 2.45 us  [project(): pl.pallas_call(proj_kernel, out_shape=(shape, shape), in_specs=[pl.BlockS...]
where the time goes in v4:
time: 154 us; the launch traced here: 153 us
  waiting for transfers between devices  43.7 us (28%)
  blocking collectives  41 us (27%)
  starting transfers between devices  27.5 us (18%)
  Pallas kernels  16.5 us (11%)
  between operations  13.6 us (9%)
  local copies, waits for them, and re-layouts  6.52 us (4%)
  other arithmetic  4.55 us (3%)
    all_to_all x1, blocking collectives, body(): lax.all_to_all(feats, ('chan',) + SEQ, split_axis=0, concat_axis=0, tiled...  41 us
    all_to_all x1, waiting for transfers between devices, body(): x = lax.all_to_all(packed, SEQ, split_axis=0, concat_axis=0, tiled=True)  39.8 us
    ppermute x4, starting transfers between devices, spread(): parts.append(lax.ppermute(wt, ('z', 'core'), pairs))  11 us
    all_to_all x1, starting transfers between devices, body(): x = lax.all_to_all(packed, SEQ, split_axis=0, concat_axis=0, tiled=True)  10.1 us
    pallas_call x1, Pallas kernels, conv_features(): pl.pallas_call(lambda *refs: conv_kernel(rows, 8, *refs), out_shape=jax.S...  8.1 us
    unnamed x20, local copies, waits for them, and re-layouts  6.52 us
    ppermute x1, starting transfers between devices, body(): halo = lax.ppermute(last, SEQ, [(i, i + 1) for i in range(groups - 1)])  4.58 us
    pallas_call x1, Pallas kernels, edges(): pl.pallas_call(edge_kernel, out_shape=jax.ShapeDtypeStruct((8, projected....  3.62 us
  transfers between devices with their start and end apart: 9, of which 3 were waited for; matrix products, arithmetic and copies ran while one was open for 2% of the time, Pallas kernels for 7%

profile of v4, /device:TPU:1, one launch (start us, length us, event | category | flops | bytes accessed | tf_op | source)
XLA Modules:
  0.0 153.4 jit_solution(16498928657156675774)
XLA Ops:
  6.5 3.6 %edges.1 = f32[8,2048]{1,0:T(8,128)} custom-call(f32[3,2048,128]{2,1,0:T(8,128)} %refs_0_.1), custom_call_target="tpu_custom_call" | custom-call | tf_op jit(solution)/shard_map/edges/pallas_call | solution.py:71
  10.2 4.6 %collective-permute-start = (f32[8,2048]{1,0:T(8,128)}, f32[8,2048]{1,0:T(8,128)S(1)}, u32[]{:S(2)}, u32[]{:S(2)}) collective-permute-start(f32[8,2048]{1,0:T(8,128)} %edges.1), channel_id=1, source_target_pairs={{0,2},{2,4},{4,6},{6,8},{8,10},{10,12},{12,14},{14,16},{16,18},{18... | collective-permute-start | bytes 196616 | tf_op jit(solution)/shard_map/ppermute | solution.py:253
  14.8 2.3 %collective-permute-start.1 = (bf16[16,4096]{1,0:T(8,128)(2,1)}, bf16[16,4096]{1,0:T(8,128)(2,1)S(1)}, u32[]{:S(2)}, u32[]{:S(2)}) collective-permute-start(bf16[16,4096]{1,0:T(8,128)(2,1)} %bitcast.24), channel_id=1, source_target_pairs={{0,0},{2,64},{64,128},{66,192},{128,2},{130,66},{192,130},{194,194... | collective-permute-start | bytes 393224 | tf_op jit(solution)/shard_map/ppermute | solution.py:212
  17.0 4.2 %collective-permute-start.2 = (bf16[16,4096]{1,0:T(8,128)(2,1)}, bf16[16,4096]{1,0:T(8,128)(2,1)S(1)}, u32[]{:S(2)}, u32[]{:S(2)}) collective-permute-start(bf16[16,4096]{1,0:T(8,128)(2,1)} %bitcast.25), channel_id=1, source_target_pairs={{0,64},{2,128},{64,192},{66,0},{128,66},{130,130},{192,194},{194,2... | collective-permute-start | bytes 393224 | tf_op jit(solution)/shard_map/ppermute | solution.py:212
  21.2 1.9 %collective-permute-start.3 = (bf16[16,4096]{1,0:T(8,128)(2,1)}, bf16[16,4096]{1,0:T(8,128)(2,1)S(1)}, u32[]{:S(2)}, u32[]{:S(2)}) collective-permute-start(bf16[16,4096]{1,0:T(8,128)(2,1)} %bitcast.26), channel_id=1, source_target_pairs={{0,128},{2,192},{64,0},{66,64},{128,130},{130,194},{192,2},{194,66... | collective-permute-start | bytes 393224 | tf_op jit(solution)/shard_map/ppermute | solution.py:212
  23.1 2.6 %collective-permute-start.4 = (bf16[16,4096]{1,0:T(8,128)(2,1)}, bf16[16,4096]{1,0:T(8,128)(2,1)S(1)}, u32[]{:S(2)}, u32[]{:S(2)}) collective-permute-start(bf16[16,4096]{1,0:T(8,128)(2,1)} %bitcast.27), channel_id=1, source_target_pairs={{0,192},{2,0},{64,64},{66,128},{128,194},{130,2},{192,66},{194,130... | collective-permute-start | bytes 393224 | tf_op jit(solution)/shard_map/ppermute | solution.py:212
  25.8 1.2 copy-done.2
  27.0 1.0 copy-done.3
  28.0 0.9 copy-done.4
  28.9 2.4 %gate_pack.1 = f32[128,48,128]{2,1,0:T(8,128)S(1)} custom-call(f32[3,2048,128]{2,1,0:T(8,128)S(1)} %copy-done, f32[8,2048]{1,0:T(8,128)S(1)} %collective-permute-done.refs_1_, f32[3,3,2048]{2,1,0:T(4,128)S(1)} %bitcast.19, f32[2048,128]{1,0:T(8,128)S(1)} %copy-done.2, bf16[96,1920]{1,0:T(8,128)(2,1)S(1)} %copy-done.3), custom_call_target="tpu_custom_call" | custom-call | flops 1000000000 | bytes 8000000 | tf_op jit(solution)/shard_map/gate_pack/pallas_call | solution.py:127
  31.3 1.4 convert_element_type.4
  32.7 0.9 pad_maximum_fusion
  33.6 10.1 %all-to-all-start = ((f16[128,48,128]{2,1,0:T(8,128)(2,1)}), f16[128,48,128]{2,1,0:T(8,128)(2,1)S(1)}, u32[]{:S(2)}, u32[]{:S(2)}) async-start(f16[128,48,128]{2,1,0:T(8,128)(2,1)} %convert_element_type.4), calls=%async_computation | async-start | bytes 3145728 | tf_op jit(solution)/shard_map/all_to_all | solution.py:260
  43.8 0.9 dynamic-slice_multiply_fusion.refs_0_
  44.6 39.8 %all-to-all-done = f16[128,48,128]{2,1,0:T(8,128)(2,1)S(1)} async-done(((f16[128,48,128]{2,1,0:T(8,128)(2,1)}), f16[128,48,128]{2,1,0:T(8,128)(2,1)S(1)}, u32[]{:S(2)}, u32[]{:S(2)}) %all-to-all-start) | async-done | bytes 1572896 | tf_op jit(solution)/shard_map/all_to_all | solution.py:260
  84.9 8.1 %conv_features.1 = bf16[2,128,16,128]{3,2,1,0:T(8,128)(2,1)S(1)} custom-call(f32[16]{0:T(128)S(1)} %dynamic-slice_multiply_fusion.refs_0_, f32[6144,128]{1,0:T(8,128)S(1)} %bitcast_convert_fusion.refs_1_, bf16[256,384]{1,0:T(8,128)(2,1)S(1)} %copy-done.7, f32[128,256]{1,0:T(8,128)S(1)} %copy-done.9, bf16[768,256]{1,0:T(8,128)(2,1)S(1)} %copy-done.5, ...), custom_call_target="tpu_custom_call" | custom-call | flops 4000000000 | bytes 6000000 | tf_op jit(solution)/shard_map/conv_features/pallas_call | solution.py:191
  93.0 41.0 %all_to_all.10 = bf16[256,16,128]{2,1,0:T(8,128)(2,1)S(1)} all-to-all(bf16[256,16,128]{2,1,0:T(8,128)(2,1)S(1)} %bitcast.18), channel_id=1, replica_groups=mesh['z'=4,'x'=4,'y'=4,'core'=2,'chan'=2] {'chan','z','x','y','core'}, dimensions={0} | all-to-all | bytes 2097152 | tf_op jit(solution)/shard_map/all_to_all | solution.py:262
  134.0 1.3 collective-permute-start.5
  135.3 2.3 %collective-permute-done.5.other = bf16[4096,128]{1,0:T(8,128)(2,1)S(1)} collective-permute-done((bf16[4096,128]{1,0:T(8,128)(2,1)S(1)}, bf16[4096,128]{1,0:T(8,128)(2,1)S(1)}, u32[]{:S(2)}, u32[]{:S(2)}) %collective-permute-start.5) | collective-permute-done | bytes 1048608 | tf_op jit(solution)/shard_map/ppermute | solution.py:266
  137.6 3.4 %copy-done.1 = bf16[64,16,4096]{2,1,0:T(8,128)(2,1)S(1)} copy-done((bf16[64,16,4096]{2,1,0:T(8,128)(2,1)S(1)}, bf16[64,16,4096]{2,1,0:T(8,128)(2,1)}, u32[]{:S(2)}) %copy-start.1) | copy-done | bytes 8388632
  141.0 2.5 %project.1 = (f32[128,1024]{1,0:T(8,128)S(1)}, f32[128,1024]{1,0:T(8,128)S(1)}) custom-call(s32[1]{0:T(128)} %bitcast.pos, bf16[4096,128]{1,0:T(8,128)(2,1)S(1)} %bitcast.17, bf16[4096,128]{1,0:T(8,128)(2,1)S(1)} %collective-permute-done.5.other, bf16[16,4,16,4096]{3,2,1,0:T(8,128)(2,1)S(1)} %bitcast.15), custom_call_target="tpu_custom_call" | custom-call | tf_op jit(solution)/shard_map/project/pallas_call | solution.py:233
  143.5 0.5 collective-permute-start.6
  143.9 1.5 %collective-permute-done.6 = f32[128,1024]{1,0:T(8,128)S(1)} collective-permute-done((f32[128,1024]{1,0:T(8,128)S(1)}, f32[128,1024]{1,0:T(8,128)S(1)}, u32[]{:S(2)}, u32[]{:S(2)}) %collective-permute-start.6) | collective-permute-done | bytes 524320 | tf_op jit(solution)/shard_map/ppermute | solution.py:268
  145.5 1.1 maximum_select_fusion
  (25 shorter events, 0.4 us)
Async XLA Ops:
  6.5 19.3 %copy-start = (f32[3,2048,128]{2,1,0:T(8,128)S(1)}, f32[3,2048,128]{2,1,0:T(8,128)}, u32[]{:S(2)}) copy-start(f32[3,2048,128]{2,1,0:T(8,128)} %refs_0_.1) | copy-start | bytes 9437188
  6.5 127.5 %all-gather.3.cloned.1.call-start = ((), (), s32[]{:S(2)}) async-start(), calls=%async_computation.2 | async-start | bytes 8912896 | tf_op jit(solution)/shard_map/all_gather | solution.py:258
  10.2 15.6 %collective-permute-start = (f32[8,2048]{1,0:T(8,128)}, f32[8,2048]{1,0:T(8,128)S(1)}, u32[]{:S(2)}, u32[]{:S(2)}) collective-permute-start(f32[8,2048]{1,0:T(8,128)} %edges.1), channel_id=1, source_target_pairs={{0,2},{2,4},{4,6},{6,8},{8,10},{10,12},{12,14},{14,16},{16,18},{18... | collective-permute-start | bytes 196616 | tf_op jit(solution)/shard_map/ppermute | solution.py:253
  14.8 17.9 %collective-permute-start.1 = (bf16[16,4096]{1,0:T(8,128)(2,1)}, bf16[16,4096]{1,0:T(8,128)(2,1)S(1)}, u32[]{:S(2)}, u32[]{:S(2)}) collective-permute-start(bf16[16,4096]{1,0:T(8,128)(2,1)} %bitcast.24), channel_id=1, source_target_pairs={{0,0},{2,64},{64,128},{66,192},{128,2},{130,66},{192,130},{194,194... | collective-permute-start | bytes 393224 | tf_op jit(solution)/shard_map/ppermute | solution.py:212
  17.0 15.7 %collective-permute-start.2 = (bf16[16,4096]{1,0:T(8,128)(2,1)}, bf16[16,4096]{1,0:T(8,128)(2,1)S(1)}, u32[]{:S(2)}, u32[]{:S(2)}) collective-permute-start(bf16[16,4096]{1,0:T(8,128)(2,1)} %bitcast.25), channel_id=1, source_target_pairs={{0,64},{2,128},{64,192},{66,0},{128,66},{130,130},{192,194},{194,2... | collective-permute-start | bytes 393224 | tf_op jit(solution)/shard_map/ppermute | solution.py:212
  21.2 11.5 %collective-permute-start.3 = (bf16[16,4096]{1,0:T(8,128)(2,1)}, bf16[16,4096]{1,0:T(8,128)(2,1)S(1)}, u32[]{:S(2)}, u32[]{:S(2)}) collective-permute-start(bf16[16,4096]{1,0:T(8,128)(2,1)} %bitcast.26), channel_id=1, source_target_pairs={{0,128},{2,192},{64,0},{66,64},{128,130},{130,194},{192,2},{194,66... | collective-permute-start | bytes 393224 | tf_op jit(solution)/shard_map/ppermute | solution.py:212
  23.1 9.6 %collective-permute-start.4 = (bf16[16,4096]{1,0:T(8,128)(2,1)}, bf16[16,4096]{1,0:T(8,128)(2,1)S(1)}, u32[]{:S(2)}, u32[]{:S(2)}) collective-permute-start(bf16[16,4096]{1,0:T(8,128)(2,1)} %bitcast.27), channel_id=1, source_target_pairs={{0,192},{2,0},{64,64},{66,128},{128,194},{130,2},{192,66},{194,130... | collective-permute-start | bytes 393224 | tf_op jit(solution)/shard_map/ppermute | solution.py:212
  25.8 1.2 copy-start.2
  27.0 1.0 copy-start.3
  28.0 0.9 copy-start.4
  33.6 50.9 %all-to-all-start = ((f16[128,48,128]{2,1,0:T(8,128)(2,1)}), f16[128,48,128]{2,1,0:T(8,128)(2,1)S(1)}, u32[]{:S(2)}, u32[]{:S(2)}) async-start(f16[128,48,128]{2,1,0:T(8,128)(2,1)} %convert_element_type.4), calls=%async_computation | async-start | bytes 3145728 | tf_op jit(solution)/shard_map/all_to_all | solution.py:260
  43.7 41.1 %copy-start.5 = (bf16[768,256]{1,0:T(8,128)(2,1)S(1)}, bf16[768,256]{1,0:T(8,128)(2,1)}, u32[]{:S(2)}) copy-start(bf16[768,256]{1,0:T(8,128)(2,1)} %constant.47.clone.refs_4_) | copy-start | bytes 1179652
  43.7 41.1 %copy-start.6 = (bf16[768,256]{1,0:T(8,128)(2,1)S(1)}, bf16[768,256]{1,0:T(8,128)(2,1)}, u32[]{:S(2)}) copy-start(bf16[768,256]{1,0:T(8,128)(2,1)} %constant.48.clone.refs_5_) | copy-start | bytes 1179652
  43.7 41.1 %copy-start.7 = (bf16[256,384]{1,0:T(8,128)(2,1)S(1)}, bf16[256,384]{1,0:T(8,128)(2,1)}, u32[]{:S(2)}) copy-start(bf16[256,384]{1,0:T(8,128)(2,1)} %constant.45.clone.refs_2_) | copy-start | bytes 589828
  43.8 41.1 %copy-start.8 = (bf16[128,768]{1,0:T(8,128)(2,1)S(1)}, bf16[128,768]{1,0:T(8,128)(2,1)}, u32[]{:S(2)}) copy-start(bf16[128,768]{1,0:T(8,128)(2,1)} %constant.49.clone.refs_6_) | copy-start | bytes 589828
  43.8 41.1 %copy-start.9 = (f32[128,256]{1,0:T(8,128)S(1)}, f32[128,256]{1,0:T(8,128)}, u32[]{:S(2)}) copy-start(f32[128,256]{1,0:T(8,128)} %constant.46.clone.refs_3_) | copy-start | bytes 393220
  134.0 3.6 %collective-permute-start.5 = (bf16[4096,128]{1,0:T(8,128)(2,1)S(1)}, bf16[4096,128]{1,0:T(8,128)(2,1)S(1)}, u32[]{:S(2)}, u32[]{:S(2)}) collective-permute-start(bf16[4096,128]{1,0:T(8,128)(2,1)S(1)} %bitcast.16), channel_id=1, source_target_pairs={{0,2},{2,0},{1,3},{3,1},{4,6},{6,4},{5,7},{7,5},{8,10},{10,8},{9,1... | collective-permute-start | bytes 3145736 | tf_op jit(solution)/shard_map/ppermute | solution.py:266
  137.6 3.4 %copy-start.1 = (bf16[64,16,4096]{2,1,0:T(8,128)(2,1)S(1)}, bf16[64,16,4096]{2,1,0:T(8,128)(2,1)}, u32[]{:S(2)}) copy-start(bf16[64,16,4096]{2,1,0:T(8,128)(2,1)} %all-gather.3.cloned.1.call-done) | copy-start | bytes 25165828
  143.5 2.0 %collective-permute-start.6 = (f32[128,1024]{1,0:T(8,128)S(1)}, f32[128,1024]{1,0:T(8,128)S(1)}, u32[]{:S(2)}, u32[]{:S(2)}) collective-permute-start(f32[128,1024]{1,0:T(8,128)S(1)} %get-tuple-element.26), channel_id=1, source_target_pairs={{0,2},{2,0},{1,3},{3,1},{4,6},{6,4},{5,7},{7,5},{8,10},{10,8},{9,1... | collective-permute-start | bytes 1572872 | tf_op jit(solution)/shard_map/ppermute | solution.py:268
Sparse Core Ops, SparseCore 0:
  33.7 97.7 all-gather.2

commit v5 on v4

--- a/solution.py
+++ b/solution.py
@@ -131,7 +131,7 @@
         out_specs=vmem,
         scratch_shapes=[pltpu.VMEM((32, slab), f32)],
         compiler_params=pltpu.CompilerParams(vmem_limit_bytes=16 * 2**20),
-        cost_estimate=pl.CostEstimate(flops=10**9, bytes_accessed=8 * 10**6, transcendentals=0),
+        cost_estimate=pl.CostEstimate(flops=8 * 10**9, bytes_accessed=8 * 10**6, transcendentals=0),
         name="gate_pack",
     )(projected, halo, taps, filters, jnp.asarray(spread_table()))
 
@@ -200,16 +200,22 @@
     )(skip, x.reshape(BLK * 3 * rows, BLK), *consts)
 
 
-def spread(w_out):
+SWAP = [(0, 1), (1, 0)]
+
+
+def chip_columns(w_out):
     wt = w_out.reshape(w_out.shape[0], -1).T
+    return jnp.concatenate([wt, lax.ppermute(wt, "core", SWAP)], axis=0)
+
+
+def spread(pair):
     parts = []
-    for k in range(4):
+    for r in range(2):
         pairs = []
         for zs in range(4):
             for cs in range(2):
-                i = (zs % 2) * 2 + cs
-                pairs.append((zs * 2 + cs, ((i + k) % 4) * 2 + zs // 2))
-        parts.append(lax.ppermute(wt, ("z", "core"), pairs))
+                pairs.append((zs * 2 + cs, ((zs + r) % 2 + 2 * cs) * 2 + zs // 2))
+        parts.append(lax.ppermute(pair, ("z", "core"), pairs))
     return parts
 
 
@@ -217,7 +223,8 @@
     chips, parts, cols, depth = w.shape
     both = jnp.concatenate([own[...], other[...]], axis=1)
     for i in range(parts):
-        k = lax.rem(pos[0] + 4 - i, 4)
+        r, h = lax.rem(pos[0] + i // 2, 2), lax.rem(pos[0] // 2 + i % 2, 2)
+        k = 2 * r + h
         t = dot(w[:, k].reshape(chips * cols, depth), both)
         acc[i // 2, :, i % 2] = t.reshape(chips, cols, 2 * BLK)
     flat = acc[...].reshape(chips * parts * cols, 2 * BLK)
@@ -249,23 +256,22 @@
     core = lax.axis_index("core")
     skip = lax.dynamic_slice(skip_gain, (me * rows,), (rows,)) / (G_SCALE * M_SCALE)
     last = edges(projected)
-    last, w_out = lax.optimization_barrier((last, w_out))
+    last, pair = lax.optimization_barrier((last, chip_columns(w_out)))
     halo = lax.ppermute(last, SEQ, [(i, i + 1) for i in range(groups - 1)])
-    parts = spread(w_out)
+    parts = spread(pair)
     taps = short_taps.transpose(0, 2, 1)
     packed = gate_pack(projected, halo, taps, filters, rows).astype(f16)
     packed, parts = lax.optimization_barrier((packed, parts))
     w = lax.all_gather(jnp.stack(parts), ("x", "y"))
-    w = w.reshape(-1, 4, w.shape[-2], w.shape[-1])
+    w = w.reshape(-1, 4, w.shape[-2] // 2, w.shape[-1])
     x = lax.all_to_all(packed, SEQ, split_axis=0, concat_axis=0, tiled=True)
     feats = conv_features(x.astype(f32), skip, rows).reshape(2 * groups, rows, count)
     mine = lax.all_to_all(feats, ("chan",) + SEQ, split_axis=0, concat_axis=0, tiled=True)
     mine = mine.reshape(2 * slab, count)
     mine, w = lax.optimization_barrier((mine, w))
-    swap = [(0, 1), (1, 0)]
-    other = lax.ppermute(mine, "core", swap)
+    other = lax.ppermute(mine, "core", SWAP)
     out_own, out_other = project(lax.axis_index("z").reshape(1), mine, other, w)
-    got = lax.ppermute(out_other, "core", swap)
+    got = lax.ppermute(out_other, "core", SWAP)
     return jnp.where(
         core == 0,
         jnp.concatenate([out_own, got], axis=1),

time: 154 us -> 152 us (0.987)
  waiting for transfers between devices: 43.7 us -> 46.3 us
  starting transfers between devices: 27.5 us -> 25.7 us
  blocking collectives: 41 us -> 39.3 us
    all_to_all x1, starting transfers between devices: 10.1 us -> 13.1 us  [body(): x = lax.all_to_all(packed, SEQ, split_axis=0, concat_axis=0, tiled=True)]
    ppermute x1, starting transfers between devices: 4.58 us -> 1.92 us  [body(): halo = lax.ppermute(last, SEQ, [(i, i + 1) for i in range(groups - 1)])]
    ppermute x6 -> x5, waiting for transfers between devices: 3.83 us -> 6.45 us  [the longest x2 2.63 us: spread(): parts.append(lax.ppermute(pair, ('z', 'core'), pairs))]
    ppermute x6 -> x5, starting transfers between devices: 12.8 us -> 10.7 us  [the longest x2 5.59 us: spread(): parts.append(lax.ppermute(pair, ('z', 'core'), pairs))]
    all_to_all x1, blocking collectives: 41 us -> 39.3 us  [body(): lax.all_to_all(feats, ('chan',) + SEQ, split_axis=0, concat_axis=0, tiled...]
    unnamed x20 -> x22, local copies, waits for them, and re-layouts: 6.52 us -> 5.63 us
  transfers between devices with their start and end apart: 9 -> 8, of which waited for: 3 -> 4; matrix products, arithmetic and copies ran while one was open for 2% -> 2% of each run, Pallas kernels for 7% -> 9%
where the time goes in v5:
time: 152 us; the launch traced here: 151 us
  waiting for transfers between devices  46.3 us (30%)
  blocking collectives  39.3 us (26%)
  starting transfers between devices  25.7 us (17%)
  Pallas kernels  16.4 us (11%)
  between operations  13.6 us (9%)
  local copies, waits for them, and re-layouts  5.63 us (4%)
  other arithmetic  4.55 us (3%)
    all_to_all x1, waiting for transfers between devices, body(): x = lax.all_to_all(packed, SEQ, split_axis=0, concat_axis=0, tiled=True)  39.9 us
    all_to_all x1, blocking collectives, body(): lax.all_to_all(feats, ('chan',) + SEQ, split_axis=0, concat_axis=0, tiled...  39.3 us
    all_to_all x1, starting transfers between devices, body(): x = lax.all_to_all(packed, SEQ, split_axis=0, concat_axis=0, tiled=True)  13.1 us
    pallas_call x1, Pallas kernels, conv_features(): pl.pallas_call(lambda *refs: conv_kernel(rows, 8, *refs), out_shape=jax.S...  8.1 us
    unnamed x22, local copies, waits for them, and re-layouts  5.63 us
    ppermute x2, starting transfers between devices, spread(): parts.append(lax.ppermute(pair, ('z', 'core'), pairs))  5.59 us
    pallas_call x1, Pallas kernels, edges(): pl.pallas_call(edge_kernel, out_shape=jax.ShapeDtypeStruct((8, projected....  3.47 us
    ppermute x1, starting transfers between devices, chip_columns(): return jnp.concatenate([wt, lax.ppermute(wt, 'core', SWAP)], axis=0)  3.32 us
  transfers between devices with their start and end apart: 8, of which 4 were waited for; matrix products, arithmetic and copies ran while one was open for 2% of the time, Pallas kernels for 9%

profile of v5, /device:TPU:1, one launch (start us, length us, event | category | flops | bytes accessed | tf_op | source)
XLA Modules:
  0.0 151.4 jit_solution(9421625388249516730)
XLA Ops:
  6.5 3.3 %collective-permute-start = (bf16[16,4096]{1,0:T(8,128)(2,1)}, bf16[16,4096]{1,0:T(8,128)(2,1)S(1)}, u32[]{:S(2)}, u32[]{:S(2)}) collective-permute-start(bf16[16,4096]{1,0:T(8,128)(2,1)} %bitcast.20), channel_id=1, source_target_pairs={{0,2},{2,0},{1,3},{3,1},{4,6},{6,4},{5,7},{7,5},{8,10},{10,8},{9,1... | collective-permute-start | bytes 393224 | tf_op jit(solution)/shard_map/ppermute | solution.py:208
  9.9 3.5 %edges.1 = f32[8,2048]{1,0:T(8,128)} custom-call(f32[3,2048,128]{2,1,0:T(8,128)} %refs_0_.1), custom_call_target="tpu_custom_call" | custom-call | tf_op jit(solution)/shard_map/edges/pallas_call | solution.py:71
  13.4 1.9 %collective-permute-start.1 = (f32[8,2048]{1,0:T(8,128)}, f32[8,2048]{1,0:T(8,128)S(1)}, u32[]{:S(2)}, u32[]{:S(2)}) collective-permute-start(f32[8,2048]{1,0:T(8,128)} %edges.1), channel_id=1, source_target_pairs={{0,2},{2,4},{4,6},{6,8},{8,10},{10,12},{12,14},{14,16},{16,18},{18... | collective-permute-start | bytes 196616 | tf_op jit(solution)/shard_map/ppermute | solution.py:260
  15.3 3.8 %collective-permute-start.2 = (bf16[32,4096]{1,0:T(8,128)(2,1)S(1)}, bf16[32,4096]{1,0:T(8,128)(2,1)S(1)}, u32[]{:S(2)}, u32[]{:S(2)}) collective-permute-start(bf16[32,4096]{1,0:T(8,128)(2,1)S(1)} %pad_maximum_fusion.1), channel_id=1, source_target_pairs={{0,0},{2,128},{64,64},{66,192},{128,2},{130,130},{192,66},{194,194... | collective-permute-start | bytes 786440 | tf_op jit(solution)/shard_map/ppermute | solution.py:218
  19.1 1.8 %collective-permute-start.3 = (bf16[32,4096]{1,0:T(8,128)(2,1)S(1)}, bf16[32,4096]{1,0:T(8,128)(2,1)S(1)}, u32[]{:S(2)}, u32[]{:S(2)}) collective-permute-start(bf16[32,4096]{1,0:T(8,128)(2,1)S(1)} %pad_maximum_fusion.1), channel_id=1, source_target_pairs={{0,64},{2,192},{64,0},{66,128},{128,66},{130,194},{192,2},{194,130... | collective-permute-start | bytes 786440 | tf_op jit(solution)/shard_map/ppermute | solution.py:218
  20.9 1.2 copy-done.2
  22.1 1.0 copy-done.6
  23.1 2.4 %gate_pack.1 = f32[128,48,128]{2,1,0:T(8,128)S(1)} custom-call(f32[3,2048,128]{2,1,0:T(8,128)S(1)} %copy-done.1, f32[8,2048]{1,0:T(8,128)S(1)} %collective-permute-done.1.refs_1_, f32[3,3,2048]{2,1,0:T(4,128)S(1)} %bitcast.17, f32[2048,128]{1,0:T(8,128)S(1)} %copy-done.2, bf16[96,1920]{1,0:T(8,128)(2,1)S(1)} %copy-done.6), custom_call_target="tpu_custom_call" | custom-call | flops 8000000000 | bytes 8000000 | tf_op jit(solution)/shard_map/gate_pack/pallas_call | solution.py:127
  25.5 1.4 convert_element_type.4
  26.9 2.6 %collective-permute-done.2 = bf16[32,4096]{1,0:T(8,128)(2,1)S(1)} collective-permute-done((bf16[32,4096]{1,0:T(8,128)(2,1)S(1)}, bf16[32,4096]{1,0:T(8,128)(2,1)S(1)}, u32[]{:S(2)}, u32[]{:S(2)}) %collective-permute-start.2) | collective-permute-done | bytes 262176 | tf_op jit(solution)/shard_map/ppermute | solution.py:218
  29.5 0.8 pad_maximum_fusion
  30.4 13.1 %all-to-all-start = ((f16[128,48,128]{2,1,0:T(8,128)(2,1)}), f16[128,48,128]{2,1,0:T(8,128)(2,1)S(1)}, u32[]{:S(2)}, u32[]{:S(2)}) async-start(f16[128,48,128]{2,1,0:T(8,128)(2,1)} %convert_element_type.4), calls=%async_computation | async-start | bytes 3145728 | tf_op jit(solution)/shard_map/all_to_all | solution.py:267
  43.5 0.9 dynamic-slice_multiply_fusion.refs_0_
  44.4 39.9 %all-to-all-done = f16[128,48,128]{2,1,0:T(8,128)(2,1)S(1)} async-done(((f16[128,48,128]{2,1,0:T(8,128)(2,1)}), f16[128,48,128]{2,1,0:T(8,128)(2,1)S(1)}, u32[]{:S(2)}, u32[]{:S(2)}) %all-to-all-start) | async-done | bytes 1572896 | tf_op jit(solution)/shard_map/all_to_all | solution.py:267
  84.2 0.3 bitcast_convert_fusion.refs_1_
  84.6 8.1 %conv_features.1 = bf16[2,128,16,128]{3,2,1,0:T(8,128)(2,1)S(1)} custom-call(f32[16]{0:T(128)S(1)} %dynamic-slice_multiply_fusion.refs_0_, f32[6144,128]{1,0:T(8,128)S(1)} %bitcast_convert_fusion.refs_1_, bf16[256,384]{1,0:T(8,128)(2,1)S(1)} %copy-done.7, f32[128,256]{1,0:T(8,128)S(1)} %copy-done.9, bf16[768,256]{1,0:T(8,128)(2,1)S(1)} %copy-done.4, ...), custom_call_target="tpu_custom_call" | custom-call | flops 4000000000 | bytes 6000000 | tf_op jit(solution)/shard_map/conv_features/pallas_call | solution.py:191
  92.7 39.3 %all_to_all.10 = bf16[256,16,128]{2,1,0:T(8,128)(2,1)S(1)} all-to-all(bf16[256,16,128]{2,1,0:T(8,128)(2,1)S(1)} %bitcast.16), channel_id=1, replica_groups=mesh['z'=4,'x'=4,'y'=4,'core'=2,'chan'=2] {'chan','z','x','y','core'}, dimensions={0} | all-to-all | bytes 2097152 | tf_op jit(solution)/shard_map/all_to_all | solution.py:269
  132.0 1.3 collective-permute-start.4
  133.3 2.3 %collective-permute-done.4.other = bf16[4096,128]{1,0:T(8,128)(2,1)S(1)} collective-permute-done((bf16[4096,128]{1,0:T(8,128)(2,1)S(1)}, bf16[4096,128]{1,0:T(8,128)(2,1)S(1)}, u32[]{:S(2)}, u32[]{:S(2)}) %collective-permute-start.4) | collective-permute-done | bytes 1048608 | tf_op jit(solution)/shard_map/ppermute | solution.py:272
  135.6 3.4 %copy-done = bf16[32,32,4096]{2,1,0:T(8,128)(2,1)S(1)} copy-done((bf16[32,32,4096]{2,1,0:T(8,128)(2,1)S(1)}, bf16[32,32,4096]{2,1,0:T(8,128)(2,1)}, u32[]{:S(2)}) %copy-start) | copy-done | bytes 8388632
  139.0 2.5 %project.1 = (f32[128,1024]{1,0:T(8,128)S(1)}, f32[128,1024]{1,0:T(8,128)S(1)}) custom-call(s32[1]{0:T(128)} %bitcast.pos, bf16[4096,128]{1,0:T(8,128)(2,1)S(1)} %bitcast.15, bf16[4096,128]{1,0:T(8,128)(2,1)S(1)} %collective-permute-done.4.other, bf16[16,4,16,4096]{3,2,1,0:T(8,128)(2,1)S(1)} %bitcast.13), custom_call_target="tpu_custom_call" | custom-call | tf_op jit(solution)/shard_map/project/pallas_call | solution.py:240
  141.5 0.5 collective-permute-start.5
  141.9 1.5 %collective-permute-done.5 = f32[128,1024]{1,0:T(8,128)S(1)} collective-permute-done((f32[128,1024]{1,0:T(8,128)S(1)}, f32[128,1024]{1,0:T(8,128)S(1)}, u32[]{:S(2)}, u32[]{:S(2)}) %collective-permute-start.5) | collective-permute-done | bytes 524320 | tf_op jit(solution)/shard_map/ppermute | solution.py:274
  143.5 1.1 maximum_select_fusion
  (26 shorter events, 0.1 us)
Async XLA Ops:
  6.5 6.8 %copy-start.10 = (bf16[4096,1,16]{0,2,1:T(8,128)(2,1)S(1)}, bf16[4096,1,16]{0,2,1:T(8,128)(2,1)}, u32[]{:S(2)}) copy-start(bf16[4096,1,16]{0,2,1:T(8,128)(2,1)} %param.15) | copy-start | bytes 393220
  6.5 14.4 %copy-start.1 = (f32[3,2048,128]{2,1,0:T(8,128)S(1)}, f32[3,2048,128]{2,1,0:T(8,128)}, u32[]{:S(2)}) copy-start(f32[3,2048,128]{2,1,0:T(8,128)} %refs_0_.1) | copy-start | bytes 9437188
  6.5 14.4 %copy-start.3 = (f32[3,2048,3]{1,2,0:T(4,128)S(1)}, f32[3,2048,3]{1,2,0:T(4,128)}, u32[]{:S(2)}) copy-start(f32[3,2048,3]{1,2,0:T(4,128)} %param.12) | copy-start | bytes 221188
  6.5 125.5 %all-gather.3.cloned.1.call-start = ((), (), s32[]{:S(2)}) async-start(), calls=%async_computation.2 | async-start | bytes 8912896 | tf_op jit(solution)/shard_map/all_gather | solution.py:265
  6.5 6.8 %collective-permute-start = (bf16[16,4096]{1,0:T(8,128)(2,1)}, bf16[16,4096]{1,0:T(8,128)(2,1)S(1)}, u32[]{:S(2)}, u32[]{:S(2)}) collective-permute-start(bf16[16,4096]{1,0:T(8,128)(2,1)} %bitcast.20), channel_id=1, source_target_pairs={{0,2},{2,0},{1,3},{3,1},{4,6},{6,4},{5,7},{7,5},{8,10},{10,8},{9,1... | collective-permute-start | bytes 393224 | tf_op jit(solution)/shard_map/ppermute | solution.py:208
  13.4 7.5 %collective-permute-start.1 = (f32[8,2048]{1,0:T(8,128)}, f32[8,2048]{1,0:T(8,128)S(1)}, u32[]{:S(2)}, u32[]{:S(2)}) collective-permute-start(f32[8,2048]{1,0:T(8,128)} %edges.1), channel_id=1, source_target_pairs={{0,2},{2,4},{4,6},{6,8},{8,10},{10,12},{12,14},{14,16},{16,18},{18... | collective-permute-start | bytes 196616 | tf_op jit(solution)/shard_map/ppermute | solution.py:260
  15.3 14.2 %collective-permute-start.2 = (bf16[32,4096]{1,0:T(8,128)(2,1)S(1)}, bf16[32,4096]{1,0:T(8,128)(2,1)S(1)}, u32[]{:S(2)}, u32[]{:S(2)}) collective-permute-start(bf16[32,4096]{1,0:T(8,128)(2,1)S(1)} %pad_maximum_fusion.1), channel_id=1, source_target_pairs={{0,0},{2,128},{64,64},{66,192},{128,2},{130,130},{192,66},{194,194... | collective-permute-start | bytes 786440 | tf_op jit(solution)/shard_map/ppermute | solution.py:218
  19.1 10.4 %collective-permute-start.3 = (bf16[32,4096]{1,0:T(8,128)(2,1)S(1)}, bf16[32,4096]{1,0:T(8,128)(2,1)S(1)}, u32[]{:S(2)}, u32[]{:S(2)}) collective-permute-start(bf16[32,4096]{1,0:T(8,128)(2,1)S(1)} %pad_maximum_fusion.1), channel_id=1, source_target_pairs={{0,64},{2,192},{64,0},{66,128},{128,66},{130,194},{192,2},{194,130... | collective-permute-start | bytes 786440 | tf_op jit(solution)/shard_map/ppermute | solution.py:218
  20.9 1.2 copy-start.2
  22.1 1.0 copy-start.6
  30.4 53.9 %all-to-all-start = ((f16[128,48,128]{2,1,0:T(8,128)(2,1)}), f16[128,48,128]{2,1,0:T(8,128)(2,1)S(1)}, u32[]{:S(2)}, u32[]{:S(2)}) async-start(f16[128,48,128]{2,1,0:T(8,128)(2,1)} %convert_element_type.4), calls=%async_computation | async-start | bytes 3145728 | tf_op jit(solution)/shard_map/all_to_all | solution.py:267
  43.5 41.1 %copy-start.4 = (bf16[768,256]{1,0:T(8,128)(2,1)S(1)}, bf16[768,256]{1,0:T(8,128)(2,1)}, u32[]{:S(2)}) copy-start(bf16[768,256]{1,0:T(8,128)(2,1)} %constant.47.clone.refs_4_) | copy-start | bytes 1179652
  43.5 41.1 %copy-start.5 = (bf16[768,256]{1,0:T(8,128)(2,1)S(1)}, bf16[768,256]{1,0:T(8,128)(2,1)}, u32[]{:S(2)}) copy-start(bf16[768,256]{1,0:T(8,128)(2,1)} %constant.48.clone.refs_5_) | copy-start | bytes 1179652
  43.5 41.1 %copy-start.7 = (bf16[256,384]{1,0:T(8,128)(2,1)S(1)}, bf16[256,384]{1,0:T(8,128)(2,1)}, u32[]{:S(2)}) copy-start(bf16[256,384]{1,0:T(8,128)(2,1)} %constant.45.clone.refs_2_) | copy-start | bytes 589828
  43.5 41.1 %copy-start.8 = (bf16[128,768]{1,0:T(8,128)(2,1)S(1)}, bf16[128,768]{1,0:T(8,128)(2,1)}, u32[]{:S(2)}) copy-start(bf16[128,768]{1,0:T(8,128)(2,1)} %constant.49.clone.refs_6_) | copy-start | bytes 589828
  43.5 41.1 %copy-start.9 = (f32[128,256]{1,0:T(8,128)S(1)}, f32[128,256]{1,0:T(8,128)}, u32[]{:S(2)}) copy-start(f32[128,256]{1,0:T(8,128)} %constant.46.clone.refs_3_) | copy-start | bytes 393220
  132.0 3.6 %collective-permute-start.4 = (bf16[4096,128]{1,0:T(8,128)(2,1)S(1)}, bf16[4096,128]{1,0:T(8,128)(2,1)S(1)}, u32[]{:S(2)}, u32[]{:S(2)}) collective-permute-start(bf16[4096,128]{1,0:T(8,128)(2,1)S(1)} %bitcast.14), channel_id=1, source_target_pairs={{0,2},{2,0},{1,3},{3,1},{4,6},{6,4},{5,7},{7,5},{8,10},{10,8},{9,1... | collective-permute-start | bytes 3145736 | tf_op jit(solution)/shard_map/ppermute | solution.py:272
  135.6 3.4 %copy-start = (bf16[32,32,4096]{2,1,0:T(8,128)(2,1)S(1)}, bf16[32,32,4096]{2,1,0:T(8,128)(2,1)}, u32[]{:S(2)}) copy-start(bf16[32,32,4096]{2,1,0:T(8,128)(2,1)} %all-gather.3.cloned.1.call-done) | copy-start | bytes 25165828
  141.5 2.0 %collective-permute-start.5 = (f32[128,1024]{1,0:T(8,128)S(1)}, f32[128,1024]{1,0:T(8,128)S(1)}, u32[]{:S(2)}, u32[]{:S(2)}) collective-permute-start(f32[128,1024]{1,0:T(8,128)S(1)} %get-tuple-element.22), channel_id=1, source_target_pairs={{0,2},{2,0},{1,3},{3,1},{4,6},{6,4},{5,7},{7,5},{8,10},{10,8},{9,1... | collective-permute-start | bytes 1572872 | tf_op jit(solution)/shard_map/ppermute | solution.py:274
Sparse Core Ops, SparseCore 0:
  30.5 98.0 all-gather.2

commit v6 on v5

--- a/solution.py
+++ b/solution.py
@@ -57,22 +57,32 @@
     return jnp.dot(a, b, preferred_element_type=f32)
 
 
-def edge_kernel(p, out):
+def edge_kernel(p, out, held, sems):
     lane = lax.broadcasted_iota(jnp.int32, (BLK, BLK), 1)
-    for q in range(0, p.shape[1], BLK):
-        x = [p[i, q : q + BLK, :] for i in range(3)]
-        x = [pltpu.roll(x[0], BLK - 4, 1), pltpu.roll(x[1], BLK - 2, 1), x[2]]
-        t = jnp.where(lane < BLK - 4, x[0], jnp.where(lane < BLK - 2, x[1], x[2]))
-        out[:, q : q + BLK] = t.T[BLK - 8 :]
+    parts = sems.shape[0]
+    per = p.shape[1] // parts
+    loads = []
+    for n in range(parts):
+        part = pl.ds(n * per, per)
+        loads.append(pltpu.make_async_copy(p.at[:, part], held.at[:, part], sems.at[n]))
+        loads[n].start()
+    for n in range(parts):
+        loads[n].wait()
+        for q in range(n * per, (n + 1) * per, BLK):
+            x = [held[i, q : q + BLK, :] for i in range(3)]
+            x = [pltpu.roll(x[0], BLK - 4, 1), pltpu.roll(x[1], BLK - 2, 1), x[2]]
+            t = jnp.where(lane < BLK - 4, x[0], jnp.where(lane < BLK - 2, x[1], x[2]))
+            out[:, q : q + BLK] = t.T[BLK - 8 :]
 
 
 def edges(projected):
-    vmem = pl.BlockSpec(memory_space=pltpu.VMEM)
     return pl.pallas_call(
         edge_kernel,
         out_shape=jax.ShapeDtypeStruct((8, projected.shape[1]), f32),
-        in_specs=[vmem],
-        out_specs=vmem,
+        in_specs=[pl.BlockSpec(memory_space=pl.ANY)],
+        out_specs=pl.BlockSpec(memory_space=pltpu.VMEM),
+        scratch_shapes=[pltpu.VMEM(projected.shape, f32), pltpu.SemaphoreType.DMA((8,))],
+        compiler_params=pltpu.CompilerParams(vmem_limit_bytes=16 * 2**20),
         name="edges",
     )(projected)
 
@@ -131,7 +141,7 @@
         out_specs=vmem,
         scratch_shapes=[pltpu.VMEM((32, slab), f32)],
         compiler_params=pltpu.CompilerParams(vmem_limit_bytes=16 * 2**20),
-        cost_estimate=pl.CostEstimate(flops=8 * 10**9, bytes_accessed=8 * 10**6, transcendentals=0),
+        cost_estimate=pl.CostEstimate(flops=10**9, bytes_accessed=8 * 10**6, transcendentals=0),
         name="gate_pack",
     )(projected, halo, taps, filters, jnp.asarray(spread_table()))
 
@@ -256,7 +266,7 @@
     core = lax.axis_index("core")
     skip = lax.dynamic_slice(skip_gain, (me * rows,), (rows,)) / (G_SCALE * M_SCALE)
     last = edges(projected)
-    last, pair = lax.optimization_barrier((last, chip_columns(w_out)))
+    pair = chip_columns(w_out)
     halo = lax.ppermute(last, SEQ, [(i, i + 1) for i in range(groups - 1)])
     parts = spread(pair)
     taps = short_taps.transpose(0, 2, 1)

time: 152 us -> 152 us (level)
    ppermute x2, waiting for transfers between devices: 2.63 us -> 0.01 us  [spread(): parts.append(lax.ppermute(pair, ('z', 'core'), pairs))]
    unnamed x22 -> x20, local copies, waits for them, and re-layouts: 5.63 us -> 5.32 us
  transfers between devices with their start and end apart: 8 -> 8, of which waited for: 4 -> 5; matrix products, arithmetic and copies ran while one was open for 2% -> 2% of each run, Pallas kernels for 9% -> 9%
where the time goes in v6:
time: 152 us
  waiting for transfers between devices  46.2 us (30%)
  blocking collectives  39.3 us (26%)
  starting transfers between devices  26.1 us (17%)
  Pallas kernels  15.8 us (10%)
  between operations  13.6 us (9%)
  other arithmetic  5.47 us (4%)
  local copies, waits for them, and re-layouts  5.32 us (4%)
    all_to_all x1, waiting for transfers between devices, body(): x = lax.all_to_all(packed, SEQ, split_axis=0, concat_axis=0, tiled=True)  39.9 us
    all_to_all x1, blocking collectives, body(): lax.all_to_all(feats, ('chan',) + SEQ, split_axis=0, concat_axis=0, tiled...  39.3 us
    all_to_all x1, starting transfers between devices, body(): x = lax.all_to_all(packed, SEQ, split_axis=0, concat_axis=0, tiled=True)  14.3 us
    pallas_call x1, Pallas kernels, conv_features(): pl.pallas_call(lambda *refs: conv_kernel(rows, 8, *refs), out_shape=jax.S...  8.1 us
    unnamed x20, local copies, waits for them, and re-layouts  5.32 us
    ppermute x2, starting transfers between devices, spread(): parts.append(lax.ppermute(pair, ('z', 'core'), pairs))  4.86 us
    ppermute x1, starting transfers between devices, chip_columns(): return jnp.concatenate([wt, lax.ppermute(wt, 'core', SWAP)], axis=0)  3.24 us
  transfers between devices with their start and end apart: 8, of which 5 were waited for; matrix products, arithmetic and copies ran while one was open for 2% of the time, Pallas kernels for 9%

profile of v6, /device:TPU:1, one launch (start us, length us, event | category | flops | bytes accessed | tf_op | source)
XLA Modules:
  0.0 151.7 jit_solution(3389300838483352282)
XLA Ops:
  6.5 3.2 %collective-permute-start.1 = (bf16[16,4096]{1,0:T(8,128)(2,1)}, bf16[16,4096]{1,0:T(8,128)(2,1)S(1)}, u32[]{:S(2)}, u32[]{:S(2)}) collective-permute-start(bf16[16,4096]{1,0:T(8,128)(2,1)} %bitcast.20), channel_id=1, source_target_pairs={{0,2},{2,0},{1,3},{3,1},{4,6},{6,4},{5,7},{7,5},{8,10},{10,8},{9,1... | collective-permute-start | bytes 393224 | tf_op jit(solution)/shard_map/ppermute | solution.py:218
  9.8 1.2 collective-permute-done.1
  11.0 0.9 pad_maximum_fusion.1
  11.9 3.4 %collective-permute-start.2 = (bf16[32,4096]{1,0:T(8,128)(2,1)S(1)}, bf16[32,4096]{1,0:T(8,128)(2,1)S(1)}, u32[]{:S(2)}, u32[]{:S(2)}) collective-permute-start(bf16[32,4096]{1,0:T(8,128)(2,1)S(1)} %pad_maximum_fusion.1), channel_id=1, source_target_pairs={{0,0},{2,128},{64,64},{66,192},{128,2},{130,130},{192,66},{194,194... | collective-permute-start | bytes 786440 | tf_op jit(solution)/shard_map/ppermute | solution.py:228
  15.3 1.5 collective-permute-start.3
  16.8 1.9 %copy-done = f32[3,2048,128]{2,1,0:T(8,128)S(1)} copy-done((f32[3,2048,128]{2,1,0:T(8,128)S(1)}, f32[3,2048,128]{2,1,0:T(8,128)}, u32[]{:S(2)}) %copy-start) | copy-done | bytes 3145752
  18.7 2.8 %edges.1 = f32[8,2048]{1,0:T(8,128)S(1)} custom-call(f32[3,2048,128]{2,1,0:T(8,128)S(1)} %copy-done), custom_call_target="tpu_custom_call" | custom-call | tf_op jit(solution)/shard_map/edges/pallas_call | solution.py:79
  21.5 1.9 %collective-permute-start = (f32[8,2048]{1,0:T(8,128)S(1)}, f32[8,2048]{1,0:T(8,128)S(1)}, u32[]{:S(2)}, u32[]{:S(2)}) collective-permute-start(f32[8,2048]{1,0:T(8,128)S(1)} %edges.1), channel_id=1, source_target_pairs={{0,2},{2,4},{4,6},{6,8},{8,10},{10,12},{12,14},{14,16},{16,18},{18... | collective-permute-start | bytes 196616 | tf_op jit(solution)/shard_map/ppermute | solution.py:270
  23.4 1.3 collective-permute-done.refs_1_
  24.8 2.4 %gate_pack.1 = f32[128,48,128]{2,1,0:T(8,128)S(1)} custom-call(f32[3,2048,128]{2,1,0:T(8,128)S(1)} %copy-done, f32[8,2048]{1,0:T(8,128)S(1)} %collective-permute-done.refs_1_, f32[3,3,2048]{2,1,0:T(4,128)S(1)} %bitcast.17, f32[2048,128]{1,0:T(8,128)S(1)} %copy-done.2, bf16[96,1920]{1,0:T(8,128)(2,1)S(1)} %copy-done.3), custom_call_target="tpu_custom_call" | custom-call | flops 1000000000 | bytes 8000000 | tf_op jit(solution)/shard_map/gate_pack/pallas_call | solution.py:137
  27.1 1.4 convert_element_type.4
  28.6 0.8 pad_maximum_fusion
  29.4 14.3 %all-to-all-start = ((f16[128,48,128]{2,1,0:T(8,128)(2,1)}), f16[128,48,128]{2,1,0:T(8,128)(2,1)S(1)}, u32[]{:S(2)}, u32[]{:S(2)}) async-start(f16[128,48,128]{2,1,0:T(8,128)(2,1)} %convert_element_type.4), calls=%async_computation | async-start | bytes 3145728 | tf_op jit(solution)/shard_map/all_to_all | solution.py:277
  43.8 0.9 dynamic-slice_multiply_fusion.refs_0_
  44.7 39.9 %all-to-all-done = f16[128,48,128]{2,1,0:T(8,128)(2,1)S(1)} async-done(((f16[128,48,128]{2,1,0:T(8,128)(2,1)}), f16[128,48,128]{2,1,0:T(8,128)(2,1)S(1)}, u32[]{:S(2)}, u32[]{:S(2)}) %all-to-all-start) | async-done | bytes 1572896 | tf_op jit(solution)/shard_map/all_to_all | solution.py:277
  84.9 8.1 %conv_features.1 = bf16[2,128,16,128]{3,2,1,0:T(8,128)(2,1)S(1)} custom-call(f32[16]{0:T(128)S(1)} %dynamic-slice_multiply_fusion.refs_0_, f32[6144,128]{1,0:T(8,128)S(1)} %bitcast_convert_fusion.refs_1_, bf16[256,384]{1,0:T(8,128)(2,1)S(1)} %copy-done.7, f32[128,256]{1,0:T(8,128)S(1)} %copy-done.9, bf16[768,256]{1,0:T(8,128)(2,1)S(1)} %copy-done.5, ...), custom_call_target="tpu_custom_call" | custom-call | flops 4000000000 | bytes 6000000 | tf_op jit(solution)/shard_map/conv_features/pallas_call | solution.py:201
  93.0 39.3 %all_to_all.10 = bf16[256,16,128]{2,1,0:T(8,128)(2,1)S(1)} all-to-all(bf16[256,16,128]{2,1,0:T(8,128)(2,1)S(1)} %bitcast.16), channel_id=1, replica_groups=mesh['z'=4,'x'=4,'y'=4,'core'=2,'chan'=2] {'chan','z','x','y','core'}, dimensions={0} | all-to-all | bytes 2097152 | tf_op jit(solution)/shard_map/all_to_all | solution.py:279
  132.3 1.3 collective-permute-start.4
  133.6 2.3 %collective-permute-done.4.other = bf16[4096,128]{1,0:T(8,128)(2,1)S(1)} collective-permute-done((bf16[4096,128]{1,0:T(8,128)(2,1)S(1)}, bf16[4096,128]{1,0:T(8,128)(2,1)S(1)}, u32[]{:S(2)}, u32[]{:S(2)}) %collective-permute-start.4) | collective-permute-done | bytes 1048608 | tf_op jit(solution)/shard_map/ppermute | solution.py:282
  135.9 3.4 %copy-done.1 = bf16[32,32,4096]{2,1,0:T(8,128)(2,1)S(1)} copy-done((bf16[32,32,4096]{2,1,0:T(8,128)(2,1)S(1)}, bf16[32,32,4096]{2,1,0:T(8,128)(2,1)}, u32[]{:S(2)}) %copy-start.1) | copy-done | bytes 8388632
  139.3 2.5 %project.1 = (f32[128,1024]{1,0:T(8,128)S(1)}, f32[128,1024]{1,0:T(8,128)S(1)}) custom-call(s32[1]{0:T(128)} %bitcast.pos, bf16[4096,128]{1,0:T(8,128)(2,1)S(1)} %bitcast.15, bf16[4096,128]{1,0:T(8,128)(2,1)S(1)} %collective-permute-done.4.other, bf16[16,4,16,4096]{3,2,1,0:T(8,128)(2,1)S(1)} %bitcast.13), custom_call_target="tpu_custom_call" | custom-call | tf_op jit(solution)/shard_map/project/pallas_call | solution.py:250
  141.8 0.5 collective-permute-start.5
  142.2 1.5 %collective-permute-done.5 = f32[128,1024]{1,0:T(8,128)S(1)} collective-permute-done((f32[128,1024]{1,0:T(8,128)S(1)}, f32[128,1024]{1,0:T(8,128)S(1)}, u32[]{:S(2)}, u32[]{:S(2)}) %collective-permute-start.5) | collective-permute-done | bytes 524320 | tf_op jit(solution)/shard_map/ppermute | solution.py:284
  143.8 1.1 maximum_select_fusion
  (24 shorter events, 0.4 us)
Async XLA Ops:
  6.5 18.2 %copy-start.3 = (bf16[96,1920]{1,0:T(8,128)(2,1)S(1)}, bf16[96,1920]{1,0:T(8,128)(2,1)}, u32[]{:S(2)}) copy-start(bf16[96,1920]{1,0:T(8,128)(2,1)} %constant.44.clone.refs_4_) | copy-start | bytes 1105924
  6.5 18.2 %copy-start.4 = (f32[3,2048,3]{1,2,0:T(4,128)S(1)}, f32[3,2048,3]{1,2,0:T(4,128)}, u32[]{:S(2)}) copy-start(f32[3,2048,3]{1,2,0:T(4,128)} %param.12) | copy-start | bytes 221188
  6.5 125.7 %all-gather.3.cloned.1.call-start = ((), (), s32[]{:S(2)}) async-start(), calls=%async_computation.2 | async-start | bytes 8912896 | tf_op jit(solution)/shard_map/all_gather | solution.py:275
  6.5 4.4 %collective-permute-start.1 = (bf16[16,4096]{1,0:T(8,128)(2,1)}, bf16[16,4096]{1,0:T(8,128)(2,1)S(1)}, u32[]{:S(2)}, u32[]{:S(2)}) collective-permute-start(bf16[16,4096]{1,0:T(8,128)(2,1)} %bitcast.20), channel_id=1, source_target_pairs={{0,2},{2,0},{1,3},{3,1},{4,6},{6,4},{5,7},{7,5},{8,10},{10,8},{9,1... | collective-permute-start | bytes 393224 | tf_op jit(solution)/shard_map/ppermute | solution.py:218
  11.9 16.6 %collective-permute-start.2 = (bf16[32,4096]{1,0:T(8,128)(2,1)S(1)}, bf16[32,4096]{1,0:T(8,128)(2,1)S(1)}, u32[]{:S(2)}, u32[]{:S(2)}) collective-permute-start(bf16[32,4096]{1,0:T(8,128)(2,1)S(1)} %pad_maximum_fusion.1), channel_id=1, source_target_pairs={{0,0},{2,128},{64,64},{66,192},{128,2},{130,130},{192,66},{194,194... | collective-permute-start | bytes 786440 | tf_op jit(solution)/shard_map/ppermute | solution.py:228
  15.3 13.2 %collective-permute-start.3 = (bf16[32,4096]{1,0:T(8,128)(2,1)S(1)}, bf16[32,4096]{1,0:T(8,128)(2,1)S(1)}, u32[]{:S(2)}, u32[]{:S(2)}) collective-permute-start(bf16[32,4096]{1,0:T(8,128)(2,1)S(1)} %pad_maximum_fusion.1), channel_id=1, source_target_pairs={{0,64},{2,192},{64,0},{66,128},{128,66},{130,194},{192,2},{194,130... | collective-permute-start | bytes 786440 | tf_op jit(solution)/shard_map/ppermute | solution.py:228
  16.8 1.9 %copy-start = (f32[3,2048,128]{2,1,0:T(8,128)S(1)}, f32[3,2048,128]{2,1,0:T(8,128)}, u32[]{:S(2)}) copy-start(f32[3,2048,128]{2,1,0:T(8,128)} %refs_0_.1) | copy-start | bytes 9437188
  18.7 6.1 %copy-start.2 = (f32[2048,128]{1,0:T(8,128)S(1)}, f32[2048,128]{1,0:T(8,128)}, u32[]{:S(2)}) copy-start(f32[2048,128]{1,0:T(8,128)} %refs_3_.2) | copy-start | bytes 3145732
  21.5 3.2 %collective-permute-start = (f32[8,2048]{1,0:T(8,128)S(1)}, f32[8,2048]{1,0:T(8,128)S(1)}, u32[]{:S(2)}, u32[]{:S(2)}) collective-permute-start(f32[8,2048]{1,0:T(8,128)S(1)} %edges.1), channel_id=1, source_target_pairs={{0,2},{2,4},{4,6},{6,8},{8,10},{10,12},{12,14},{14,16},{16,18},{18... | collective-permute-start | bytes 196616 | tf_op jit(solution)/shard_map/ppermute | solution.py:270
  29.4 55.1 %all-to-all-start = ((f16[128,48,128]{2,1,0:T(8,128)(2,1)}), f16[128,48,128]{2,1,0:T(8,128)(2,1)S(1)}, u32[]{:S(2)}, u32[]{:S(2)}) async-start(f16[128,48,128]{2,1,0:T(8,128)(2,1)} %convert_element_type.4), calls=%async_computation | async-start | bytes 3145728 | tf_op jit(solution)/shard_map/all_to_all | solution.py:277
  43.7 41.1 %copy-start.5 = (bf16[768,256]{1,0:T(8,128)(2,1)S(1)}, bf16[768,256]{1,0:T(8,128)(2,1)}, u32[]{:S(2)}) copy-start(bf16[768,256]{1,0:T(8,128)(2,1)} %constant.47.clone.refs_4_) | copy-start | bytes 1179652
  43.7 41.1 %copy-start.6 = (bf16[768,256]{1,0:T(8,128)(2,1)S(1)}, bf16[768,256]{1,0:T(8,128)(2,1)}, u32[]{:S(2)}) copy-start(bf16[768,256]{1,0:T(8,128)(2,1)} %constant.48.clone.refs_5_) | copy-start | bytes 1179652
  43.8 41.1 %copy-start.7 = (bf16[256,384]{1,0:T(8,128)(2,1)S(1)}, bf16[256,384]{1,0:T(8,128)(2,1)}, u32[]{:S(2)}) copy-start(bf16[256,384]{1,0:T(8,128)(2,1)} %constant.45.clone.refs_2_) | copy-start | bytes 589828
  43.8 41.1 %copy-start.8 = (bf16[128,768]{1,0:T(8,128)(2,1)S(1)}, bf16[128,768]{1,0:T(8,128)(2,1)}, u32[]{:S(2)}) copy-start(bf16[128,768]{1,0:T(8,128)(2,1)} %constant.49.clone.refs_6_) | copy-start | bytes 589828
  43.8 41.1 %copy-start.9 = (f32[128,256]{1,0:T(8,128)S(1)}, f32[128,256]{1,0:T(8,128)}, u32[]{:S(2)}) copy-start(f32[128,256]{1,0:T(8,128)} %constant.46.clone.refs_3_) | copy-start | bytes 393220
  132.3 3.6 %collective-permute-start.4 = (bf16[4096,128]{1,0:T(8,128)(2,1)S(1)}, bf16[4096,128]{1,0:T(8,128)(2,1)S(1)}, u32[]{:S(2)}, u32[]{:S(2)}) collective-permute-start(bf16[4096,128]{1,0:T(8,128)(2,1)S(1)} %bitcast.14), channel_id=1, source_target_pairs={{0,2},{2,0},{1,3},{3,1},{4,6},{6,4},{5,7},{7,5},{8,10},{10,8},{9,1... | collective-permute-start | bytes 3145736 | tf_op jit(solution)/shard_map/ppermute | solution.py:282
  135.9 3.4 %copy-start.1 = (bf16[32,32,4096]{2,1,0:T(8,128)(2,1)S(1)}, bf16[32,32,4096]{2,1,0:T(8,128)(2,1)}, u32[]{:S(2)}) copy-start(bf16[32,32,4096]{2,1,0:T(8,128)(2,1)} %all-gather.3.cloned.1.call-done) | copy-start | bytes 25165828
  141.8 2.0 %collective-permute-start.5 = (f32[128,1024]{1,0:T(8,128)S(1)}, f32[128,1024]{1,0:T(8,128)S(1)}, u32[]{:S(2)}, u32[]{:S(2)}) collective-permute-start(f32[128,1024]{1,0:T(8,128)S(1)} %get-tuple-element.18), channel_id=1, source_target_pairs={{0,2},{2,0},{1,3},{3,1},{4,6},{6,4},{5,7},{7,5},{8,10},{10,8},{9,1... | collective-permute-start | bytes 1572872 | tf_op jit(solution)/shard_map/ppermute | solution.py:284
Sparse Core Ops, SparseCore 0:
  29.5 98.9 all-gather.2
